TPU v7x, 256 devices: a whole 4x4x8 slice. The times are simulated.
256 devices in a mesh: week: 32 (over z, y), region: 8 (over x, core).
Axes of the slice: x: 4, y: 4, z: 8, core: 2. Of those that a mesh axis runs over, the one named last changes fastest.
Arguments:
- stock_start: float32 [128, 8, 32768], P('week', 'region'), may hold values from 0 to 2
- ship_start: float32 [128, 8, 32768], P('week', 'region'), may hold values from 0 to 1
- dual_start: float32 [128, 8, 32768], P('week', 'region'), may hold values from -12 to 12
- demand: float32 [128, 8, 32768], P('week', 'region'), may hold values from 0.2 to 6
- cost_hold: float32 [128, 8, 32768], P('week', 'region'), may hold values from 0.2 to 6
- cost_ship: float32 [128, 8, 32768], P('week', 'region'), may hold values from 0.2 to 6
- ship_cap: int32 [128, 8, 32768], P('week', 'region'), may hold values from 1 to 3
- lead_weeks: int32 [8, 32768], P('region'), may hold values from 1 to 2
- lane_mix: float32 [8, 128, 128], P('region'), may hold values from 0 to 1, as said below
Outputs:
- stock_final: float32 [128, 8, 32768], P('week', 'region')
- ship_final: float32 [128, 8, 32768], P('week', 'region')
- dual_final: float32 [128, 8, 32768], P('week', 'region')
- projected: float32 [128, 8, 32768], P('week', 'region')
Inputs may be any that keep to these rules, and one draw needn't show every extreme that they name: `lane_mix`: nonnegative shares.
All inputs are finite; a program needn't handle non-finite values.
Results may differ from a plain program's by a relative error of at most 0.0001.
Values sent between devices are 32-bit elements; how exact they have to be, the bound alone decides.
A program may use at most 64 MiB of HBM per device.

v0:
```python
import jax
import jax.numpy as jnp
from jax import lax
from jax.sharding import PartitionSpec as P

LEAD_MAX = 2
PANEL = 128
ITERS = 2


step_eta = 0.25
eps_move = 1e-06


def passed_along(block, axis, distance):
    devices = range(lax.axis_size(axis))
    route = [(i - distance, i) for i in devices if i - distance in devices]
    return lax.ppermute(block, axis, route)


def shifted(block, axis, distance):
    devices = range(lax.axis_size(axis))
    route = [((i - distance) % len(devices), i) for i in devices]
    return lax.ppermute(block, axis, route)


def prefix(part, axis, combine, identity):
    place = lax.axis_index(axis)
    gathered = lax.all_gather(part, axis)
    state = jnp.zeros_like(part) + jnp.asarray(identity, part.dtype)

    def one(turn, state):
        return combine(state, lax.dynamic_index_in_dim(gathered, turn, 0, False))

    return lax.fori_loop(0, place, one, state)


def add_terms(earlier, later_term):
    return earlier + later_term


def shards(
    stock_start,
    ship_start,
    dual_start,
    demand,
    cost_hold,
    cost_ship,
    ship_cap,
    lead_weeks,
    lane_mix,
):
    stock_level = stock_start[:, 0, :]
    ship_flow = ship_start[:, 0, :]
    dual_price = dual_start[:, 0, :]
    demand_rows = demand[:, 0, :]
    hold_rows = cost_hold[:, 0, :]
    ship_rows = cost_ship[:, 0, :]
    cap_float = ship_cap[:, 0, :].astype(jnp.float32)
    lead_row = lead_weeks[0][None]
    mix_local = lane_mix[0]
    week_rows = stock_level.shape[0]

    def panel_mix(values_in, transpose):
        panels_view = values_in.reshape(values_in.shape[0], -1, PANEL)
        if transpose:
            mixed = jnp.einsum(
                "wbj,kj->wbk", panels_view, mix_local, precision=lax.Precision.HIGHEST
            )
        else:
            mixed = jnp.einsum(
                "wbk,kj->wbj", panels_view, mix_local, precision=lax.Precision.HIGHEST
            )
        return mixed.reshape(values_in.shape)

    def forward(stock_now, ship_now):
        ship_below, stock_below = passed_along((ship_now[-LEAD_MAX:], stock_now[-1:]), "week", 1)
        ship_ext = jnp.concatenate([ship_below, ship_now], axis=0)
        lagged = jnp.zeros_like(ship_now)
        for offset in range(1, LEAD_MAX + 1):
            lagged = lagged + jnp.where(
                lead_row == offset, ship_ext[LEAD_MAX - offset : LEAD_MAX - offset + week_rows], 0.0
            )
        receipts = shifted(panel_mix(lagged, False), "region", 1)
        previous = jnp.concatenate([stock_below, stock_now[:-1]], axis=0)
        return (stock_now - previous + ship_now - receipts, receipts)

    def adjoint(dual_now):
        pulled = panel_mix(shifted(dual_now, "region", -1), True)
        upper_rows, pulled_upper = passed_along(
            (dual_now[:LEAD_MAX], pulled[:LEAD_MAX]), "week", -1
        )
        dual_ext = jnp.concatenate([dual_now, upper_rows], axis=0)
        pulled_ext = jnp.concatenate([pulled, pulled_upper], axis=0)
        picked = jnp.zeros_like(dual_now)
        for offset in range(1, LEAD_MAX + 1):
            picked = picked + jnp.where(
                lead_row == offset, pulled_ext[offset : offset + week_rows], 0.0
            )
        return (dual_now - dual_ext[1 : week_rows + 1], dual_now - picked)

    balance, receipts = forward(stock_level, ship_flow)
    grad_hold, grad_ship = adjoint(dual_price)
    primal_step = step_eta
    dual_step = step_eta
    for round_index in range(ITERS):
        new_stock = jnp.maximum(
            stock_level - primal_step * (cost_hold[:, 0, :] * 0.0 + hold_rows - grad_hold), 0.0
        )
        new_ship = jnp.clip(ship_flow - primal_step * (ship_rows - grad_ship), 0.0, cap_float)
        if round_index == 0:
            local_primal = jnp.sum((new_stock - stock_level) ** 2) + jnp.sum(
                (new_ship - ship_flow) ** 2
            )
            moved_primal = lax.psum(local_primal, ("week", "region"))
        new_balance, receipts = forward(new_stock, new_ship)
        new_dual = dual_price + dual_step * (demand_rows - 2.0 * new_balance + balance)
        if round_index == 0:
            local_dual = jnp.sum((new_dual - dual_price) ** 2)
            moved_dual = lax.psum(local_dual, ("week", "region"))
            weight = jnp.sqrt(jnp.sqrt((moved_dual + eps_move) / (moved_primal + eps_move)))
            primal_step = step_eta / weight
            dual_step = step_eta * weight
        if round_index + 1 < ITERS:
            grad_hold, grad_ship = adjoint(new_dual)
        stock_level, ship_flow, dual_price, balance = (new_stock, new_ship, new_dual, new_balance)
    net_flow = receipts - ship_flow - demand_rows
    totals = jnp.sum(net_flow, axis=0)
    before = prefix(totals, "week", add_terms, jnp.zeros_like(totals))
    projected = before[None] + jnp.cumsum(net_flow, axis=0)
    return (
        stock_level[:, None, :],
        ship_flow[:, None, :],
        dual_price[:, None, :],
        projected[:, None, :],
    )


def solution(mesh):
    in_specs = (
        P("week", "region", None),
        P("week", "region", None),
        P("week", "region", None),
        P("week", "region", None),
        P("week", "region", None),
        P("week", "region", None),
        P("week", "region", None),
        P("region", None),
        P("region", None, None),
    )
    out_specs = (
        P("week", "region", None),
        P("week", "region", None),
        P("week", "region", None),
        P("week", "region", None),
    )
    return jax.shard_map(shards, mesh=mesh, in_specs=in_specs, out_specs=out_specs, check_vma=False)
```

profile of v0, /device:TPU:248, one launch (start us, length us, event | category | flops | bytes accessed | tf_op | source)
XLA Modules:
  0.0 322.1 jit_solution(10816970265212063367)
XLA Ops:
  8.8 2.2 collective-permute-start.2
  11.0 6.7 %collective-permute-done.2 = f32[4,32768]{1,0:T(4,128)S(1)} collective-permute-done((f32[4,32768]{1,0:T(4,128)S(1)}, f32[4,32768]{1,0:T(4,128)S(1)}, u32[]{:S(2)}, u32[]{:S(2)}) %collective-permute-start.2) | collective-permute-done | bytes 524320 | tf_op jit(solution)/shard_map/ppermute | solution.py:24
  18.6 2.7 collective-permute-start.3
  24.9 1.6 collective-permute-done.3
  26.5 2.4 multiply_reduce_fusion
  30.6 5.2 %collective-permute-start = (f32[2,32768]{1,0:T(2,128)S(1)}, f32[2,32768]{1,0:T(2,128)S(1)}, u32[]{:S(2)}, u32[]{:S(2)}) collective-permute-start(f32[2,32768]{1,0:T(2,128)S(1)} %bitcast.159), channel_id=1, source_target_pairs={{8,0},{16,8},{24,16},{32,24},{40,32},{48,40},{56,48},{64,56},{72,6... | collective-permute-start | bytes 786440 | tf_op jit(solution)/shard_map/ppermute | solution.py:18
  36.1 2.4 collective-permute-done.4
  41.5 1.9 collective-permute-start.8
  44.7 1.6 fusion.68
  48.2 2.9 collective-permute-done.6
  51.1 3.7 %collective-permute-done.1 = f32[1,32768]{1,0:T(1,128)S(1)} collective-permute-done((f32[1,32768]{1,0:T(1,128)S(1)}, f32[1,32768]{1,0:T(1,128)S(1)}, u32[]{:S(2)}, u32[]{:S(2)}) %collective-permute-start.1) | collective-permute-done | bytes 131104 | tf_op jit(solution)/shard_map/ppermute | solution.py:18
  56.0 3.4 %multiply_reduce_fusion.1 = (f32[]{:T(128)}, f32[4,32768]{1,0:T(4,128)S(1)}, f32[4,32768]{1,0:T(4,128)}) fusion(f32[4,1,32768]{2,1,0:T(1,128)S(1)} %copy-done.2, f32[4,32768]{1,0:T(4,128)S(1)} %collective-permute-done.8, f32[4,1,32768]{2,1,0:T(1,128)S(1)} %copy-done.1, f32[3,32768]{1,0:T(4,128)S(1)} %bitcast.153, f32[1,32768]{1,0:T(1,128)S(1)} %collective-permute-done.6, ...), kind=kLoop, calls=%fused_computation.110 | loop fusion | flops 2097151 | bytes 6291460 | tf_op jit(solution)/shard_map/reduce_sum | solution.py:119
  60.2 3.6 %collective-permute-start.9 = (f32[2,32768]{1,0:T(2,128)}, f32[2,32768]{1,0:T(2,128)S(1)}, u32[]{:S(2)}, u32[]{:S(2)}) collective-permute-start(f32[2,32768]{1,0:T(2,128)} %slice.134), channel_id=1, source_target_pairs={{8,0},{16,8},{24,16},{32,24},{40,32},{48,40},{56,48},{64,56},{72,6... | collective-permute-start | bytes 786440 | tf_op jit(solution)/shard_map/ppermute | solution.py:18
  63.8 2.3 collective-permute-done.10
  66.9 3.6 %collective-permute-start.11 = (f32[2,32768]{1,0:T(2,128)S(1)}, f32[2,32768]{1,0:T(2,128)S(1)}, u32[]{:S(2)}, u32[]{:S(2)}) collective-permute-start(f32[2,32768]{1,0:T(2,128)S(1)} %bitcast.160), channel_id=1, source_target_pairs={{8,0},{16,8},{24,16},{32,24},{40,32},{48,40},{56,48},{64,56},{72,6... | collective-permute-start | bytes 786440 | tf_op jit(solution)/shard_map/ppermute | solution.py:18
  71.8 80.5 %all-reduce = (f32[]{:T(128)}, f32[]{:T(128)}) all-reduce(f32[]{:T(128)} %get-tuple-element.46, f32[]{:T(128)S(6)} %add.87), channel_id=1, replica_groups=mesh['week'=32,'region'=8] {'week','region'}, use_global_device_ids=true, to_apply=%region_1.2 | all-reduce | flops 2 | bytes 16 | tf_op jit(solution)/shard_map/psum | solution.py:120
  154.9 3.3 %bitcast_minimum_fusion = (f32[4,32768]{1,0:T(4,128)S(1)}, f32[4,32768]{1,0:T(4,128)S(1)}) fusion(f32[4,32768]{1,0:T(4,128)S(1)} %get-tuple-element.43, f32[4,32768]{1,0:T(4,128)S(1)} %get-tuple-element.47, f32[2,32768]{1,0:T(2,128)} %copy-done.10, f32[4,32768]{1,0:T(4,128)S(1)} %bitcast.154, s32[4,1,32768]{2,1,0:T(1,128)} %param.17, ...), kind=kLoop, calls=%fused_computation.106 | loop fusion | flops 2621440 | bytes 5308420 | tf_op jit(solution)/shard_map/jit(clip)/min | solution.py:110
  159.7 8.6 %collective-permute-done.13 = f32[2,32768]{1,0:T(2,128)S(1)} collective-permute-done((f32[2,32768]{1,0:T(2,128)S(1)}, f32[2,32768]{1,0:T(2,128)S(1)}, u32[]{:S(2)}, u32[]{:S(2)}) %collective-permute-start.13) | collective-permute-done | bytes 262176 | tf_op jit(solution)/shard_map/ppermute | solution.py:18
  172.1 5.6 %collective-permute-done.12 = f32[1,32768]{1,0:T(1,128)S(1)} collective-permute-done((f32[1,32768]{1,0:T(1,128)S(1)}, f32[1,32768]{1,0:T(1,128)S(1)}, u32[]{:S(2)}, u32[]{:S(2)}) %collective-permute-start.12) | collective-permute-done | bytes 131104 | tf_op jit(solution)/shard_map/ppermute | solution.py:18
  177.6 3.0 collective-permute-done.14
  181.4 3.0 fusion.74
  188.2 77.9 %all-gather.3.cloned.1.call-done = f32[1048576]{0:T(1024)} async-done(((f32[32768]{0:T(1024)}), f32[1048576]{0:T(1024)}) %all-gather.3.cloned.1.call-update) | async-done | bytes 4194320 | tf_op jit(solution)/shard_map/all_gather | solution.py:29
  266.2 4.9 %reshape.81 = f32[32,32768]{1,0:T(8,128)} reshape(f32[1048576]{0:T(1024)} %all-gather.3.cloned.1.call-done) | data formatting | bytes 8388608 | tf_op jit(solution)/shard_map/all_gather | solution.py:29
  271.1 42.9 %while.10 = (s32[]{:T(128)}, f32[32768]{0:T(1024)S(1)}, s32[]{:T(128)}, f32[32,32768]{1,0:T(8,128)}, s32[]{:T(128)}, /*index=5*/s32[]{:T(128)}, s32[]{:T(128)}) while((s32[]{:T(128)}, f32[32768]{0:T(1024)S(1)}, s32[]{:T(128)}, f32[32,32768]{1,0:T(8,128)}, s32[]{:T(128)}, /*index=5*/s32[]{:T(128)}, s32[]{:T(128)}) %tuple.31), condition=%wide.region_7.8_spmd, body=%wide.region_6.7_spmd.sunk | while | flops 32773 | bytes 655475 | solution.py:35
  (142 shorter events, 70.9 us)
Async XLA Ops:
  7.2 19.3 %copy-start.2 = (f32[4,1,32768]{2,1,0:T(1,128)S(1)}, f32[4,1,32768]{2,1,0:T(1,128)}, u32[]{:S(2)}) copy-start(f32[4,1,32768]{2,1,0:T(1,128)} %param.13) | copy-start | bytes 1572868
  7.2 19.3 %copy-start.1 = (f32[4,1,32768]{2,1,0:T(1,128)S(1)}, f32[4,1,32768]{2,1,0:T(1,128)}, u32[]{:S(2)}) copy-start(f32[4,1,32768]{2,1,0:T(1,128)} %param.12) | copy-start | bytes 1572868
  7.2 16.5 %copy-start.11 = (s32[1,32768]{1,0:T(1,128)S(1)}, s32[1,32768]{1,0:T(1,128)}, u32[]{:S(2)}) copy-start(s32[1,32768]{1,0:T(1,128)} %param.18) | copy-start | bytes 393220
  7.2 19.3 %copy-start.7 = (f32[4,1,32768]{2,1,0:T(1,128)S(1)}, f32[4,1,32768]{2,1,0:T(1,128)}, u32[]{:S(2)}) copy-start(f32[4,1,32768]{2,1,0:T(1,128)} %param.16) | copy-start | bytes 1572868
  7.2 19.3 %copy-start.8 = (s32[4,1,32768]{2,1,0:T(1,128)S(1)}, s32[4,1,32768]{2,1,0:T(1,128)}, u32[]{:S(2)}) copy-start(s32[4,1,32768]{2,1,0:T(1,128)} %param.17) | copy-start | bytes 1572868
  7.2 258.9 %all-gather.3.cloned.1.call-start = ((), (), s32[]{:S(2)}) async-start(), calls=%async_computation | async-start | bytes 4325376 | tf_op jit(solution)/shard_map/all_gather | solution.py:29
  8.8 8.9 %collective-permute-start.2 = (f32[4,32768]{1,0:T(4,128)S(1)}, f32[4,32768]{1,0:T(4,128)S(1)}, u32[]{:S(2)}, u32[]{:S(2)}) collective-permute-start(f32[4,32768]{1,0:T(4,128)S(1)} %bitcast.149), channel_id=1, source_target_pairs={{1,0},{2,1},{3,2},{4,3},{5,4},{6,5},{7,6},{0,7},{9,8},{10,9},{11,1... | collective-permute-start | bytes 1572872 | tf_op jit(solution)/shard_map/ppermute | solution.py:24
  18.6 7.9 %collective-permute-start.3 = (f32[2,32768]{1,0:T(2,128)S(1)}, f32[2,32768]{1,0:T(2,128)S(1)}, u32[]{:S(2)}, u32[]{:S(2)}) collective-permute-start(f32[2,32768]{1,0:T(2,128)S(1)} %bitcast.162), channel_id=1, source_target_pairs={{8,0},{16,8},{24,16},{32,24},{40,32},{48,40},{56,48},{64,56},{72,6... | collective-permute-start | bytes 786440 | tf_op jit(solution)/shard_map/ppermute | solution.py:18
  22.4 13.7 %collective-permute-start.7 = (f32[2,32768]{1,0:T(2,128)S(1)}, f32[2,32768]{1,0:T(2,128)S(1)}, u32[]{:S(2)}, u32[]{:S(2)}) collective-permute-start(f32[2,32768]{1,0:T(2,128)S(1)} %bitcast.161), channel_id=1, source_target_pairs={{0,8},{8,16},{16,24},{24,32},{32,40},{40,48},{48,56},{56,64},{64,7... | collective-permute-start | bytes 786440 | tf_op jit(solution)/shard_map/ppermute | solution.py:18
  29.0 9.5 %collective-permute-start.4 = (f32[2,32768]{1,0:T(2,128)S(1)}, f32[2,32768]{1,0:T(2,128)S(1)}, u32[]{:S(2)}, u32[]{:S(2)}) collective-permute-start(f32[2,32768]{1,0:T(2,128)S(1)} %slice.129), channel_id=1, source_target_pairs={{0,8},{8,16},{16,24},{24,32},{32,40},{40,48},{48,56},{56,64},{64,7... | collective-permute-start | bytes 786440 | tf_op jit(solution)/shard_map/ppermute | solution.py:18
  30.6 14.1 %copy-start.4 = (f32[4,1,32768]{2,1,0:T(1,128)S(1)}, f32[4,1,32768]{2,1,0:T(1,128)}, u32[]{:S(2)}) copy-start(f32[4,1,32768]{2,1,0:T(1,128)} %param.15) | copy-start | bytes 1572868
  30.6 14.1 %collective-permute-start = (f32[2,32768]{1,0:T(2,128)S(1)}, f32[2,32768]{1,0:T(2,128)S(1)}, u32[]{:S(2)}, u32[]{:S(2)}) collective-permute-start(f32[2,32768]{1,0:T(2,128)S(1)} %bitcast.159), channel_id=1, source_target_pairs={{8,0},{16,8},{24,16},{32,24},{40,32},{48,40},{56,48},{64,56},{72,6... | collective-permute-start | bytes 786440 | tf_op jit(solution)/shard_map/ppermute | solution.py:18
  39.6 16.4 %copy-start.5 = (f32[4,1,32768]{2,1,0:T(1,128)S(1)}, f32[4,1,32768]{2,1,0:T(1,128)}, u32[]{:S(2)}) copy-start(f32[4,1,32768]{2,1,0:T(1,128)} %param.14) | copy-start | bytes 1572868
  40.6 14.2 %collective-permute-start.5 = (f32[4,32768]{1,0:T(4,128)S(1)}, f32[4,32768]{1,0:T(4,128)S(1)}, u32[]{:S(2)}, u32[]{:S(2)}) collective-permute-start(f32[4,32768]{1,0:T(4,128)S(1)} %bitcast.155), channel_id=1, source_target_pairs={{7,0},{0,1},{1,2},{2,3},{3,4},{4,5},{5,6},{6,7},{15,8},{8,9},{9,10... | collective-permute-start | bytes 1572872 | tf_op jit(solution)/shard_map/ppermute | solution.py:24
  41.5 14.5 %collective-permute-start.8 = (f32[4,32768]{1,0:T(4,128)S(1)}, f32[4,32768]{1,0:T(4,128)S(1)}, u32[]{:S(2)}, u32[]{:S(2)}) collective-permute-start(f32[4,32768]{1,0:T(4,128)S(1)} %bitcast.156), channel_id=1, source_target_pairs={{7,0},{0,1},{1,2},{2,3},{3,4},{4,5},{5,6},{6,7},{15,8},{8,9},{9,10... | collective-permute-start | bytes 1572872 | tf_op jit(solution)/shard_map/ppermute | solution.py:24
  43.4 7.7 %collective-permute-start.6 = (f32[1,32768]{1,0:T(1,128)S(1)}, f32[1,32768]{1,0:T(1,128)S(1)}, u32[]{:S(2)}, u32[]{:S(2)}) collective-permute-start(f32[1,32768]{1,0:T(1,128)S(1)} %slice_bitcast_fusion.2), channel_id=1, source_target_pairs={{0,8},{8,16},{16,24},{24,32},{32,40},{40,48},{48,56},{56,64},{64,7... | collective-permute-start | bytes 393224 | tf_op jit(solution)/shard_map/ppermute | solution.py:18
  46.4 8.3 %collective-permute-start.1 = (f32[1,32768]{1,0:T(1,128)S(1)}, f32[1,32768]{1,0:T(1,128)S(1)}, u32[]{:S(2)}, u32[]{:S(2)}) collective-permute-start(f32[1,32768]{1,0:T(1,128)S(1)} %slice.124), channel_id=1, source_target_pairs={{0,8},{8,16},{16,24},{24,32},{32,40},{40,48},{48,56},{56,64},{64,7... | collective-permute-start | bytes 393224 | tf_op jit(solution)/shard_map/ppermute | solution.py:18
  59.4 6.7 %collective-permute-start.10 = (f32[4,32768]{1,0:T(4,128)S(1)}, f32[4,32768]{1,0:T(4,128)S(1)}, u32[]{:S(2)}, u32[]{:S(2)}) collective-permute-start(f32[4,32768]{1,0:T(4,128)S(1)} %get-tuple-element.47), channel_id=1, source_target_pairs={{1,0},{2,1},{3,2},{4,3},{5,4},{6,5},{7,6},{0,7},{9,8},{10,9},{11,1... | collective-permute-start | bytes 1572872 | tf_op jit(solution)/shard_map/ppermute | solution.py:24
  60.2 94.0 %collective-permute-start.9 = (f32[2,32768]{1,0:T(2,128)}, f32[2,32768]{1,0:T(2,128)S(1)}, u32[]{:S(2)}, u32[]{:S(2)}) collective-permute-start(f32[2,32768]{1,0:T(2,128)} %slice.134), channel_id=1, source_target_pairs={{8,0},{16,8},{24,16},{32,24},{40,32},{48,40},{56,48},{64,56},{72,6... | collective-permute-start | bytes 786440 | tf_op jit(solution)/shard_map/ppermute | solution.py:18
  66.9 87.3 %collective-permute-start.11 = (f32[2,32768]{1,0:T(2,128)S(1)}, f32[2,32768]{1,0:T(2,128)S(1)}, u32[]{:S(2)}, u32[]{:S(2)}) collective-permute-start(f32[2,32768]{1,0:T(2,128)S(1)} %bitcast.160), channel_id=1, source_target_pairs={{8,0},{16,8},{24,16},{32,24},{40,32},{48,40},{56,48},{64,56},{72,6... | collective-permute-start | bytes 786440 | tf_op jit(solution)/shard_map/ppermute | solution.py:18
  158.2 23.2 %copy-start.6 = (f32[4,1,32768]{2,1,0:T(1,128)S(1)}, f32[4,1,32768]{2,1,0:T(1,128)}, u32[]{:S(2)}) copy-start(f32[4,1,32768]{2,1,0:T(1,128)} %param.14) | copy-start | bytes 1572868
  158.4 9.9 %collective-permute-start.13 = (f32[2,32768]{1,0:T(2,128)S(1)}, f32[2,32768]{1,0:T(2,128)S(1)}, u32[]{:S(2)}, u32[]{:S(2)}) collective-permute-start(f32[2,32768]{1,0:T(2,128)S(1)} %slice.140), channel_id=1, source_target_pairs={{0,8},{8,16},{16,24},{24,32},{32,40},{40,48},{48,56},{56,64},{64,7... | collective-permute-start | bytes 786440 | tf_op jit(solution)/shard_map/ppermute | solution.py:18
  170.6 10.0 %collective-permute-start.14 = (f32[4,32768]{1,0:T(4,128)}, f32[4,32768]{1,0:T(4,128)S(1)}, u32[]{:S(2)}, u32[]{:S(2)}) collective-permute-start(f32[4,32768]{1,0:T(4,128)} %bitcast.128), channel_id=1, source_target_pairs={{7,0},{0,1},{1,2},{2,3},{3,4},{4,5},{5,6},{6,7},{15,8},{8,9},{9,10... | collective-permute-start | bytes 1572872 | tf_op jit(solution)/shard_map/ppermute | solution.py:24
  170.7 6.9 %collective-permute-start.12 = (f32[1,32768]{1,0:T(1,128)S(1)}, f32[1,32768]{1,0:T(1,128)S(1)}, u32[]{:S(2)}, u32[]{:S(2)}) collective-permute-start(f32[1,32768]{1,0:T(1,128)S(1)} %slice.138), channel_id=1, source_target_pairs={{0,8},{8,16},{16,24},{24,32},{32,40},{40,48},{48,56},{56,64},{64,7... | collective-permute-start | bytes 393224 | tf_op jit(solution)/shard_map/ppermute | solution.py:18
  (6 other events, 45.4 us)
Sparse Core Ops, SparseCore 0:
  184.5 81.6 all-gather.2
where the time goes:
time: 324 us; the launch traced here: 322 us
  waiting for transfers between devices  116 us (36%)
  blocking collectives  80.5 us (25%)
  local copies, waits for them, and re-layouts  59.1 us (18%)
  starting transfers between devices  27.2 us (8%)
  other arithmetic  18.1 us (6%)
  between operations  17.3 us (5%)
    psum x1, blocking collectives, shards(): moved_dual = lax.psum(local_dual, ('week', 'region'))  80.5 us
    all_gather x1, waiting for transfers between devices, prefix(): gathered = lax.all_gather(part, axis)  77.9 us
    dynamic_slice x31, local copies, waits for them, and re-layouts, one(): return combine(state, lax.dynamic_index_in_dim(gathered, turn, 0, False))  41 us
    ppermute x10, waiting for transfers between devices, passed_along(): return lax.ppermute(block, axis, route)  24.8 us
    ppermute x10, starting transfers between devices, passed_along(): return lax.ppermute(block, axis, route)  23 us
    ppermute x5, waiting for transfers between devices, shifted(): return lax.ppermute(block, axis, route)  13.2 us
    unnamed x38, local copies, waits for them, and re-layouts  7.04 us
  transfers between devices with their start and end apart: 16, of which 11 were waited for; matrix products, arithmetic and copies ran while one was open for 5% of the time, Pallas kernels for 0%

commit v1 on v0

v1 whole, which is shorter than its diff:
```python
import functools

import jax
import jax.numpy as jnp
from jax import lax
from jax.experimental import pallas as pl
from jax.experimental.pallas import tpu as pltpu
from jax.sharding import PartitionSpec as P

PANEL = 128
ROWS = 4
CHUNKS = 4
LAG = 2
STEP_ETA = 0.25
EPS_MOVE = 1e-06
MESH = pl.DeviceIdType.MESH
F32 = jnp.float32
BF16 = jnp.bfloat16


def ring_distance(d, n):
    return min(d % n, -d % n)


def week_offsets(weeks):
    def hops(d):
        return ring_distance(d // 4, max(weeks // 4, 1)) + ring_distance(d % 4, 4)

    return sorted(range(1, weeks), key=lambda d: (-hops(d), d))


def kernel(weeks, regions, panels, *refs):
    (
        stock_in, ship_in, dual_in, demand_in, hold_in, cost_in, cap_in, lead_in, mix_in,
        stock_out, ship_out, dual_out, proj_out,
        v0, s0, y0, dem, ch, cs, cap, lead, mixw,
        w_fwd, w_adj,
        v1, s1, y1, v2, s2, y2, bal1, pj,
        yb0, yo0, yb1, yo1,
        fs_t, fv_t, fb_t, fh_t,
        fs_1, fb_1, fh_1,
        fs_2, fb_2, fh_2,
        m_send, m_recv, s_sum, net, a1, a2, pref,
        row1, rows1, row2, rows2,
        load_sem, out_sem,
        y0_ss, y0_rs, y1_ss, y1_rs, ft_ss, ft_rs, f1_ss, f1_rs, f2_ss, f2_rs,
        m_ss, m_rs, r1_ss, r1_rs, r2_ss, r2_rs, p1_ss, p1_rs, p2_ss, p2_rs,
    ) = refs
    w = lax.axis_index("week")
    r = lax.axis_index("region")
    first = w == 0
    last = w == weeks - 1
    size = panels // CHUNKS
    piece = panels // weeks

    def there(dw, dr):
        return (lax.rem(w + dw + weeks, weeks), lax.rem(r + dr + regions, regions))

    loads = []
    for k, (src, dst) in enumerate(
        (
            (dual_in, y0), (mix_in, mixw), (lead_in, lead), (stock_in, v0), (ship_in, s0),
            (hold_in, ch), (cost_in, cs), (cap_in, cap), (demand_in, dem),
        )
    ):
        cp = pltpu.make_async_copy(src, dst, load_sem.at[k])
        cp.start()
        loads.append(cp)

    w_off = week_offsets(weeks)
    near = [(0, 1), (1, 1), (1, 0), (0, -1), (-1, -1), (-1, 0)]
    far = [(d, 0) for d in w_off] + [(0, d) for d in range(1, regions)]
    partners = list(dict.fromkeys((a % weeks, b % regions) for a, b in near + far))
    barrier = pltpu.get_barrier_semaphore()
    for dw, dr in partners:
        pl.semaphore_signal(barrier, inc=1, device_id=there(dw, dr), device_id_type=MESH)
    pl.semaphore_wait(barrier, len(partners))

    sends = []

    def send(src, dst, ss, rs, to):
        cp = pltpu.make_async_remote_copy(
            src_ref=src, dst_ref=dst, send_sem=ss, recv_sem=rs, device_id=to, device_id_type=MESH
        )
        cp.start()
        sends.append(cp)
        return cp

    def span(c):
        return pl.ds(c * size, size)

    def send_prices(y, yb, yo, ss, rs, c):
        k = 3 * c
        return [
            send(y.at[0:2, span(c)], yb.at[3:5, span(c)], ss.at[k], rs.at[k], there(-1, -1)),
            send(y.at[0:1, span(c)], yo.at[:, span(c)], ss.at[k + 1], rs.at[k + 1], there(-1, 0)),
            send(y.at[1:4, span(c)], yb.at[0:3, span(c)], ss.at[k + 2], rs.at[k + 2], there(0, -1)),
        ]

    def send_arrivals(fs, fv, fb, fh, ss, rs, c):
        k = 3 * c
        return [
            send(fs.at[3:5, span(c)], fb.at[3:5, span(c)], ss.at[k], rs.at[k], there(1, 1)),
            send(fv, fh.at[:, span(c)], ss.at[k + 1], rs.at[k + 1], there(1, 0)),
            send(fs.at[0:3, span(c)], fb.at[0:3, span(c)], ss.at[k + 2], rs.at[k + 2], there(0, 1)),
        ]

    def mix(values, weight):
        hi = values.astype(BF16)
        lo = (values - hi.astype(F32)).astype(BF16)
        both = jnp.dot(jnp.concatenate([hi, lo], axis=1), weight[...], preferred_element_type=F32)
        return both[:, :PANEL] + both[:, PANEL:]

    def pulled_gradients(y, yb, yo, c):
        pulled = mix(yb[:, span(c), :].reshape(5 * size, PANEL), w_adj).reshape(5, size, PANEL)
        pulled = [pulled[k] for k in range(5)]
        pulled[3] = jnp.where(last, 0.0, pulled[3])
        pulled[4] = jnp.where(last, 0.0, pulled[4])
        short = lead[span(c), :] == 1
        rows = [y[t, span(c), :] for t in range(ROWS)]
        after = rows[1:] + [jnp.where(last, 0.0, yo[0, span(c), :])]
        grad_v = [rows[t] - after[t] for t in range(ROWS)]
        grad_s = [rows[t] - jnp.where(short, pulled[t], pulled[t + 1]) for t in range(ROWS)]
        return grad_v, grad_s

    def mix_arrivals(rows, fs, c):
        short = lead[span(c), :] == 1
        lagged = jnp.concatenate(
            [
                jnp.where(short, rows[0], 0.0),
                jnp.where(short, rows[1], rows[0]),
                jnp.where(short, rows[2], rows[1]),
                jnp.where(short, rows[3], rows[2]),
                jnp.where(short, 0.0, rows[3]),
            ],
            axis=0,
        )
        fs[:, span(c), :] = mix(lagged, w_fwd).reshape(5, size, PANEL)

    def arrivals(fb, c):
        early = [jnp.where(first, 0.0, fb[3 + k, span(c), :]) for k in range(2)]
        own = [fb[k, span(c), :] for k in range(3)]
        return early, [early[0], own[0] + early[1], own[1], own[2]]

    def balance_of(v_rows, s_rows, fh, receipts, c):
        before = [jnp.where(first, 0.0, fh[0, span(c), :])] + v_rows[:-1]
        return [v_rows[t] - before[t] + s_rows[t] - receipts[t] for t in range(ROWS)]

    def fold(values):
        return jnp.sum(values.reshape(size // 8, 8, PANEL), axis=0)

    loads[0].wait()
    y0_cp = [send_prices(y0, yb0, yo0, y0_ss, y0_rs, c) for c in range(CHUNKS)]
    loads[1].wait()
    for weight, dest in ((mixw[...], w_fwd), (mixw[...].T, w_adj)):
        hi = weight.astype(BF16)
        lo = (weight - hi.astype(F32)).astype(BF16)
        half = jnp.concatenate([hi, lo], axis=1)
        dest[...] = jnp.concatenate([half, half], axis=0)
    for cp in loads[2:]:
        cp.wait()

    primal = jnp.zeros((8, PANEL), F32)
    dual = jnp.zeros((8, PANEL), F32)
    ft_cp = {}
    y1_cp = {}

    def first_primal(c, primal):
        for cp in y0_cp[c]:
            cp.wait_recv()
        grad_v, grad_s = pulled_gradients(y0, yb0, yo0, c)
        ahead = []
        for t in range(ROWS):
            old_v = v0[t, span(c), :]
            new_v = jnp.maximum(old_v - STEP_ETA * (ch[t, span(c), :] - grad_v[t]), 0.0)
            v1[t, span(c), :] = new_v
            if t == ROWS - 1:
                fv_t[0, span(c), :] = 2.0 * new_v - old_v
            old_s = s0[t, span(c), :]
            top = cap[t, span(c), :].astype(F32)
            new_s = jnp.minimum(
                jnp.maximum(old_s - STEP_ETA * (cs[t, span(c), :] - grad_s[t]), 0.0), top
            )
            s1[t, span(c), :] = new_s
            primal = primal + fold((new_v - old_v) ** 2) + fold((new_s - old_s) ** 2)
            ahead.append(2.0 * new_s - old_s)
        mix_arrivals(ahead, fs_t, c)
        ft_cp[c] = send_arrivals(fs_t, fv_t.at[:, span(c)], fb_t, fh_t, ft_ss, ft_rs, c)
        return primal

    def first_dual(c, dual):
        for cp in ft_cp[c]:
            cp.wait_recv()
        _, receipts = arrivals(fb_t, c)
        v_rows = [2.0 * v1[t, span(c), :] - v0[t, span(c), :] for t in range(ROWS)]
        s_rows = [2.0 * s1[t, span(c), :] - s0[t, span(c), :] for t in range(ROWS)]
        ahead = balance_of(v_rows, s_rows, fh_t, receipts, c)
        for t in range(ROWS):
            moved = STEP_ETA * (dem[t, span(c), :] - ahead[t])
            new_y = y0[t, span(c), :] + moved
            y1[t, span(c), :] = new_y
            dual = dual + fold((new_y - y0[t, span(c), :]) ** 2)
        if c < CHUNKS - 1:
            y1_cp[c] = send_prices(y1, yb1, yo1, y1_ss, y1_rs, c)
        return dual

    for c in range(CHUNKS + LAG):
        if c < CHUNKS:
            primal = first_primal(c, primal)
        if c >= LAG:
            dual = first_dual(c - LAG, dual)

    lane = lax.broadcasted_iota(jnp.int32, (1, PANEL), 1)
    primal = jnp.sum(primal, axis=0, keepdims=True)
    dual = jnp.sum(dual, axis=0, keepdims=True)
    half = PANEL // 2
    mine = jnp.where(
        lane < half, primal + pltpu.roll(primal, half, 1), dual + pltpu.roll(dual, half, 1)
    )
    row1[...] = mine
    r1_cp = [
        send(row1, rows1.at[w], r1_ss.at[d], r1_rs.at[d], there(d, 0)) for d in w_off
    ]
    rows1[w] = mine
    c = CHUNKS - 1
    y1_cp[c] = send_prices(y1, yb1, yo1, y1_ss, y1_rs, c)

    f1_cp = []
    for c in range(CHUNKS):
        mix_arrivals([s1[t, span(c), :] for t in range(ROWS)], fs_1, c)
        f1_cp.append(send_arrivals(fs_1, v1.at[3:4, span(c)], fb_1, fh_1, f1_ss, f1_rs, c))

    for cp in r1_cp:
        cp.wait_recv()
    mine = jnp.sum(rows1[...], axis=0)
    row2[...] = mine
    r2_cp = [
        send(row2, rows2.at[r], r2_ss.at[d], r2_rs.at[d], there(0, d)) for d in range(1, regions)
    ]
    rows2[r] = mine

    for c in range(CHUNKS):
        for cp in y1_cp[c]:
            cp.wait_recv()
        grad_v, grad_s = pulled_gradients(y1, yb1, yo1, c)
        for t in range(ROWS):
            ch[t, span(c), :] = ch[t, span(c), :] - grad_v[t]
            cs[t, span(c), :] = cs[t, span(c), :] - grad_s[t]

    for cp in r2_cp:
        cp.wait_recv()
    total = jnp.sum(rows2[...], axis=0)
    moved_primal = jnp.sum(jnp.where(lane < half, total, 0.0), axis=1, keepdims=True)
    moved_dual = jnp.sum(jnp.where(lane < half, 0.0, total), axis=1, keepdims=True)
    ratio = jnp.broadcast_to((moved_dual + EPS_MOVE) / (moved_primal + EPS_MOVE), (1, PANEL))
    weight = jnp.sqrt(jnp.sqrt(ratio))
    primal_step = STEP_ETA / weight
    dual_step = STEP_ETA * weight

    m_cp = []
    for c in range(CHUNKS):
        sums = jnp.zeros((size, PANEL), F32)
        for t in range(ROWS):
            v2[t, span(c), :] = jnp.maximum(v1[t, span(c), :] - primal_step * ch[t, span(c), :], 0.0)
            new_s = jnp.minimum(
                jnp.maximum(s1[t, span(c), :] - primal_step * cs[t, span(c), :], 0.0),
                cap[t, span(c), :].astype(F32),
            )
            s2[t, span(c), :] = new_s
            sums = sums + new_s
        s_sum[span(c), :] = sums
        m_send[span(c), :] = mix(sums, w_fwd)
        m_cp.append(
            send(m_send.at[span(c)], m_recv.at[span(c)], m_ss.at[c], m_rs.at[c], there(0, 1))
        )
    outs = [
        pltpu.make_async_copy(v2, stock_out, out_sem.at[0]),
        pltpu.make_async_copy(s2, ship_out, out_sem.at[1]),
    ]
    for cp in outs:
        cp.start()

    f2_cp = []

    def last_arrivals(c):
        mix_arrivals([s2[t, span(c), :] for t in range(ROWS)], fs_2, c)
        f2_cp.append(send_arrivals(fs_2, v2.at[3:4, span(c)], fb_2, fh_2, f2_ss, f2_rs, c))

    for c in range(CHUNKS):
        last_arrivals(c)

    for c in range(CHUNKS):
        m_cp[c].wait_recv()
        sums = m_recv[span(c), :] - s_sum[span(c), :]
        for t in range(ROWS):
            sums = sums - dem[t, span(c), :]
        net[span(c), :] = sums
    p1_cp = []
    for d in w_off:
        to = there(d, 0)
        p1_cp.append(
            send(net.at[pl.ds(to[0] * piece, piece)], a1.at[w], p1_ss.at[d], p1_rs.at[d], to)
        )
    a1[w] = net[pl.ds(w * piece, piece), :]

    for c in range(CHUNKS):
        for cp in f1_cp[c]:
            cp.wait_recv()
        _, receipts = arrivals(fb_1, c)
        v_rows = [v1[t, span(c), :] for t in range(ROWS)]
        s_rows = [s1[t, span(c), :] for t in range(ROWS)]
        rows = balance_of(v_rows, s_rows, fh_1, receipts, c)
        for t in range(ROWS):
            bal1[t, span(c), :] = rows[t]

    for cp in p1_cp:
        cp.wait_recv()
    running = jnp.zeros((piece, PANEL), F32)
    for k in range(weeks):
        a2[k] = running
        running = running + a1[k]
    p2_cp = []
    for d in w_off:
        to = there(d, 0)
        p2_cp.append(
            send(a2.at[to[0]], pref.at[pl.ds(w * piece, piece)], p2_ss.at[d], p2_rs.at[d], to)
        )
    pref[pl.ds(w * piece, piece), :] = a2[w]

    for c in range(CHUNKS):
        for cp in f2_cp[c]:
            cp.wait_recv()
        early, receipts = arrivals(fb_2, c)
        v_rows = [v2[t, span(c), :] for t in range(ROWS)]
        s_rows = [s2[t, span(c), :] for t in range(ROWS)]
        rows = balance_of(v_rows, s_rows, fh_2, receipts, c)
        flow = -early[0] - early[1]
        for t in range(ROWS):
            wanted = dem[t, span(c), :]
            y2[t, span(c), :] = y1[t, span(c), :] + dual_step * (
                wanted - 2.0 * rows[t] + bal1[t, span(c), :]
            )
            flow = flow + (receipts[t] - s_rows[t] - wanted)
            pj[t, span(c), :] = flow
    outs.append(pltpu.make_async_copy(y2, dual_out, out_sem.at[2]))
    outs[-1].start()

    for cp in p2_cp:
        cp.wait_recv()
    for t in range(ROWS):
        pj[t] = pj[t] + pref[...]
    outs.append(pltpu.make_async_copy(pj, proj_out, out_sem.at[3]))
    outs[-1].start()
    for cp in sends:
        cp.wait_send()
    for cp in outs:
        cp.wait()


def shards(weeks, regions, stock, ship, dual, demand, hold, cost, cap, lead, mix):
    items = stock.shape[-1]
    panels = items // PANEL

    def view(a):
        return a.reshape(ROWS, panels, PANEL)

    slab = (ROWS, panels, PANEL)

    def vmem(*shape, dtype=F32):
        return pltpu.VMEM(shape, dtype)

    def sems(n):
        return [pltpu.SemaphoreType.DMA((n,))] * 2

    exchange = [vmem(5, panels, PANEL), vmem(5, panels, PANEL), vmem(1, panels, PANEL)]
    scratch = (
        [vmem(*slab)] * 6
        + [vmem(*slab, dtype=jnp.int32), vmem(panels, PANEL, dtype=jnp.int32), vmem(PANEL, PANEL)]
        + [vmem(2 * PANEL, 2 * PANEL, dtype=BF16)] * 2
        + [vmem(*slab)] * 8
        + [vmem(5, panels, PANEL), vmem(1, panels, PANEL)] * 2
        + [vmem(5, panels, PANEL), vmem(1, panels, PANEL)] * 2
        + exchange
        + exchange
        + [vmem(panels, PANEL)] * 4
        + [vmem(weeks, panels // weeks, PANEL)] * 2
        + [vmem(panels, PANEL)]
        + [vmem(1, PANEL), vmem(weeks, 1, PANEL), vmem(1, PANEL), vmem(regions, 1, PANEL)]
        + [pltpu.SemaphoreType.DMA((9,)), pltpu.SemaphoreType.DMA((4,))]
        + sems(3 * CHUNKS) * 5
        + sems(CHUNKS)
        + sems(weeks)
        + sems(regions)
        + sems(weeks) * 2
    )
    outs = pl.pallas_call(
        functools.partial(kernel, weeks, regions, panels),
        out_shape=[jax.ShapeDtypeStruct(slab, F32)] * 4,
        in_specs=[pl.BlockSpec(memory_space=pl.ANY)] * 9,
        out_specs=[pl.BlockSpec(memory_space=pl.ANY)] * 4,
        scratch_shapes=scratch,
        compiler_params=pltpu.CompilerParams(
            collective_id=0, has_side_effects=True, vmem_limit_bytes=48 * 1024 * 1024
        ),
        cost_estimate=pl.CostEstimate(
            flops=2 * 6 * 5 * 5 * panels * PANEL * PANEL,
            bytes_accessed=12 * 4 * ROWS * panels * PANEL,
            transcendentals=0,
        ),
        name="primal_dual",
    )(
        view(stock), view(ship), view(dual), view(demand), view(hold), view(cost), view(cap),
        lead.reshape(panels, PANEL), mix.reshape(PANEL, PANEL),
    )
    return tuple(o.reshape(ROWS, 1, items) for o in outs)


def solution(mesh):
    block = P("week", "region", None)
    in_specs = (block,) * 7 + (P("region", None), P("region", None, None))
    body = functools.partial(shards, mesh.shape["week"], mesh.shape["region"])
    return jax.shard_map(
        body, mesh=mesh, in_specs=in_specs, out_specs=(block,) * 4, check_vma=False
    )
```

time: 324 us -> 78.5 us (0.24)
  the two profiles are of different devices: /device:TPU:248 before, /device:TPU:2 now
where the time goes in v1:
time: 78.5 us; the launch traced here: 78.1 us
  Pallas kernels  65.2 us (83%)
  local copies, waits for them, and re-layouts  12.2 us (16%)
    pallas_call x1, Pallas kernels, shards(): pl.pallas_call(functools.partial(kernel, weeks, regions, panels), out_sha...  65.2 us
    unnamed x22, local copies, waits for them, and re-layouts  12.2 us

profile of v1, /device:TPU:2, one launch (start us, length us, event | category | flops | bytes accessed | tf_op | source)
XLA Modules:
  0.0 78.1 jit_solution(13955162391236095909)
XLA Ops:
  0.6 0.0 copy-start
  0.6 1.0 %copy-done = f32[4,1,32768]{2,1,0:T(1,128)S(1)} copy-done((f32[4,1,32768]{2,1,0:T(1,128)S(1)}, f32[4,1,32768]{2,1,0:T(1,128)}, u32[]{:S(2)}) %copy-start) | copy-done | bytes 524312
  1.7 0.0 copy-start.1
  1.7 1.0 %copy-done.1 = f32[4,1,32768]{2,1,0:T(1,128)S(1)} copy-done((f32[4,1,32768]{2,1,0:T(1,128)S(1)}, f32[4,1,32768]{2,1,0:T(1,128)}, u32[]{:S(2)}) %copy-start.1) | copy-done | bytes 524312
  2.7 0.0 copy-start.2
  2.7 1.0 %copy-done.2 = f32[4,1,32768]{2,1,0:T(1,128)S(1)} copy-done((f32[4,1,32768]{2,1,0:T(1,128)S(1)}, f32[4,1,32768]{2,1,0:T(1,128)}, u32[]{:S(2)}) %copy-start.2) | copy-done | bytes 524312
  3.8 0.0 copy-start.3
  3.8 1.0 %copy-done.3 = f32[4,1,32768]{2,1,0:T(1,128)S(1)} copy-done((f32[4,1,32768]{2,1,0:T(1,128)S(1)}, f32[4,1,32768]{2,1,0:T(1,128)}, u32[]{:S(2)}) %copy-start.3) | copy-done | bytes 524312
  4.8 0.0 copy-start.4
  4.8 1.0 %copy-done.4 = f32[4,1,32768]{2,1,0:T(1,128)S(1)} copy-done((f32[4,1,32768]{2,1,0:T(1,128)S(1)}, f32[4,1,32768]{2,1,0:T(1,128)}, u32[]{:S(2)}) %copy-start.4) | copy-done | bytes 524312
  5.8 0.0 copy-start.5
  5.8 1.0 %copy-done.5 = f32[4,1,32768]{2,1,0:T(1,128)S(1)} copy-done((f32[4,1,32768]{2,1,0:T(1,128)S(1)}, f32[4,1,32768]{2,1,0:T(1,128)}, u32[]{:S(2)}) %copy-start.5) | copy-done | bytes 524312
  6.9 0.0 copy-start.6
  6.9 1.0 %copy-done.6 = s32[4,1,32768]{2,1,0:T(1,128)S(1)} copy-done((s32[4,1,32768]{2,1,0:T(1,128)S(1)}, s32[4,1,32768]{2,1,0:T(1,128)}, u32[]{:S(2)}) %copy-start.6) | copy-done | bytes 524312
  7.9 0.0 copy-start.7
  7.9 0.9 %copy-done.7 = s32[1,32768]{1,0:T(1,128)S(1)} copy-done((s32[1,32768]{1,0:T(1,128)S(1)}, s32[1,32768]{1,0:T(1,128)}, u32[]{:S(2)}) %copy-start.7) | copy-done | bytes 131096
  8.8 0.0 copy-start.8
  8.8 0.8 %copy-done.8 = f32[1,128,128]{2,1,0:T(8,128)S(1)} copy-done((f32[1,128,128]{2,1,0:T(8,128)S(1)}, f32[1,128,128]{2,1,0:T(8,128)}, u32[]{:S(2)}) %copy-start.8) | copy-done | bytes 65560
  9.7 65.2 %primal_dual.1 = (f32[4,256,128]{2,1,0:T(8,128)S(1)}, f32[4,256,128]{2,1,0:T(8,128)S(1)}, f32[4,256,128]{2,1,0:T(8,128)S(1)}, f32[4,256,128]{2,1,0:T(8,128)S(1)}) custom-call(f32[4,256,128]{2,1,0:T(8,128)S(1)} %bitcast.17, f32[4,256,128]{2,1,0:T(8,128)S(1)} %bitcast.18, f32[4,256,128]{2,1,0:T(8,128)S(1)} %bitcast.19, f32[4,256,128]{2,1,0:T(8,128)S(1)} %bitcast.20, ...), custom_call_target="tpu_custom_call" | custom-call | flops 1258291200 | bytes 6291456 | tf_op jit(solution)/shard_map/primal_dual/pallas_call | solution.py:396
  74.9 0.8 %copy.21 = f32[4,1,32768]{2,1,0:T(1,128)} copy(f32[4,1,32768]{2,1,0:T(1,128)S(1)} %bitcast.16) | data formatting | bytes 1048576
  75.7 0.8 %copy.22 = f32[4,1,32768]{2,1,0:T(1,128)} copy(f32[4,1,32768]{2,1,0:T(1,128)S(1)} %bitcast.15) | data formatting | bytes 1048576
  76.5 0.8 %copy.23 = f32[4,1,32768]{2,1,0:T(1,128)} copy(f32[4,1,32768]{2,1,0:T(1,128)S(1)} %bitcast.14) | data formatting | bytes 1048576
  77.3 0.8 %copy.24 = f32[4,1,32768]{2,1,0:T(1,128)} copy(f32[4,1,32768]{2,1,0:T(1,128)S(1)} %bitcast.13) | data formatting | bytes 1048576
Async XLA Ops:
  0.6 1.0 %copy-start = (f32[4,1,32768]{2,1,0:T(1,128)S(1)}, f32[4,1,32768]{2,1,0:T(1,128)}, u32[]{:S(2)}) copy-start(f32[4,1,32768]{2,1,0:T(1,128)} %param.9) | copy-start | bytes 1572868
  1.7 1.0 %copy-start.1 = (f32[4,1,32768]{2,1,0:T(1,128)S(1)}, f32[4,1,32768]{2,1,0:T(1,128)}, u32[]{:S(2)}) copy-start(f32[4,1,32768]{2,1,0:T(1,128)} %param.10) | copy-start | bytes 1572868
  2.7 1.0 %copy-start.2 = (f32[4,1,32768]{2,1,0:T(1,128)S(1)}, f32[4,1,32768]{2,1,0:T(1,128)}, u32[]{:S(2)}) copy-start(f32[4,1,32768]{2,1,0:T(1,128)} %param.11) | copy-start | bytes 1572868
  3.8 1.0 %copy-start.3 = (f32[4,1,32768]{2,1,0:T(1,128)S(1)}, f32[4,1,32768]{2,1,0:T(1,128)}, u32[]{:S(2)}) copy-start(f32[4,1,32768]{2,1,0:T(1,128)} %param.12) | copy-start | bytes 1572868
  4.8 1.0 %copy-start.4 = (f32[4,1,32768]{2,1,0:T(1,128)S(1)}, f32[4,1,32768]{2,1,0:T(1,128)}, u32[]{:S(2)}) copy-start(f32[4,1,32768]{2,1,0:T(1,128)} %param.13) | copy-start | bytes 1572868
  5.8 1.0 %copy-start.5 = (f32[4,1,32768]{2,1,0:T(1,128)S(1)}, f32[4,1,32768]{2,1,0:T(1,128)}, u32[]{:S(2)}) copy-start(f32[4,1,32768]{2,1,0:T(1,128)} %param.14) | copy-start | bytes 1572868
  6.9 1.0 %copy-start.6 = (s32[4,1,32768]{2,1,0:T(1,128)S(1)}, s32[4,1,32768]{2,1,0:T(1,128)}, u32[]{:S(2)}) copy-start(s32[4,1,32768]{2,1,0:T(1,128)} %param.15) | copy-start | bytes 1572868
  7.9 0.9 %copy-start.7 = (s32[1,32768]{1,0:T(1,128)S(1)}, s32[1,32768]{1,0:T(1,128)}, u32[]{:S(2)}) copy-start(s32[1,32768]{1,0:T(1,128)} %param.16) | copy-start | bytes 393220
  8.8 0.8 %copy-start.8 = (f32[1,128,128]{2,1,0:T(8,128)S(1)}, f32[1,128,128]{2,1,0:T(8,128)}, u32[]{:S(2)}) copy-start(f32[1,128,128]{2,1,0:T(8,128)} %param.17) | copy-start | bytes 196612

commit v2 on v1

--- a/solution.py
+++ b/solution.py
@@ -32,17 +32,17 @@
 def kernel(weeks, regions, panels, *refs):
     (
         stock_in, ship_in, dual_in, demand_in, hold_in, cost_in, cap_in, lead_in, mix_in,
-        stock_out, ship_out, dual_out, proj_out,
+        v2, s2, y2, pj, pref,
         v0, s0, y0, dem, ch, cs, cap, lead, mixw,
         w_fwd, w_adj,
-        v1, s1, y1, v2, s2, y2, bal1, pj,
+        v1, s1, y1, bal1,
         yb0, yo0, yb1, yo1,
         fs_t, fv_t, fb_t, fh_t,
         fs_1, fb_1, fh_1,
         fs_2, fb_2, fh_2,
-        m_send, m_recv, s_sum, net, a1, a2, pref,
+        m_send, m_recv, s_sum, net, a1, a2,
         row1, rows1, row2, rows2,
-        load_sem, out_sem,
+        load_sem,
         y0_ss, y0_rs, y1_ss, y1_rs, ft_ss, ft_rs, f1_ss, f1_rs, f2_ss, f2_rs,
         m_ss, m_rs, r1_ss, r1_rs, r2_ss, r2_rs, p1_ss, p1_rs, p2_ss, p2_rs,
     ) = refs
@@ -59,7 +59,7 @@
     loads = []
     for k, (src, dst) in enumerate(
         (
-            (dual_in, y0), (mix_in, mixw), (lead_in, lead), (stock_in, v0), (ship_in, s0),
+            (dual_in, y0), (mix_in, mixw), (lead_in, lead), (ship_in, s0), (stock_in, v0),
             (hold_in, ch), (cost_in, cs), (cap_in, cap), (demand_in, dem),
         )
     ):
@@ -74,8 +74,6 @@
     barrier = pltpu.get_barrier_semaphore()
     for dw, dr in partners:
         pl.semaphore_signal(barrier, inc=1, device_id=there(dw, dr), device_id_type=MESH)
-    pl.semaphore_wait(barrier, len(partners))
-
     sends = []
 
     def send(src, dst, ss, rs, to):
@@ -149,15 +147,28 @@
     def fold(values):
         return jnp.sum(values.reshape(size // 8, 8, PANEL), axis=0)
 
-    loads[0].wait()
-    y0_cp = [send_prices(y0, yb0, yo0, y0_ss, y0_rs, c) for c in range(CHUNKS)]
     loads[1].wait()
     for weight, dest in ((mixw[...], w_fwd), (mixw[...].T, w_adj)):
         hi = weight.astype(BF16)
         lo = (weight - hi.astype(F32)).astype(BF16)
         half = jnp.concatenate([hi, lo], axis=1)
         dest[...] = jnp.concatenate([half, half], axis=0)
-    for cp in loads[2:]:
+    f1_cp = {}
+    for cp in loads[2:5]:
+        cp.wait()
+    for c in range(CHUNKS):
+        mix_arrivals([s0[t, span(c), :] for t in range(ROWS)], fs_1, c)
+    loads[0].wait()
+
+    def send_start(c):
+        f1_cp[c] = send_arrivals(fs_1, v0.at[3:4, span(c)], fb_1, fh_1, f1_ss, f1_rs, c)
+
+    pl.semaphore_wait(barrier, len(partners))
+
+    y0_cp = [send_prices(y0, yb0, yo0, y0_ss, y0_rs, c) for c in range(CHUNKS)]
+    for c in range(CHUNKS // 2):
+        send_start(c)
+    for cp in loads[5:]:
         cp.wait()
 
     primal = jnp.zeros((8, PANEL), F32)
@@ -196,6 +207,7 @@
         s_rows = [2.0 * s1[t, span(c), :] - s0[t, span(c), :] for t in range(ROWS)]
         ahead = balance_of(v_rows, s_rows, fh_t, receipts, c)
         for t in range(ROWS):
+            bal1[t, span(c), :] = ahead[t]
             moved = STEP_ETA * (dem[t, span(c), :] - ahead[t])
             new_y = y0[t, span(c), :] + moved
             y1[t, span(c), :] = new_y
@@ -207,6 +219,9 @@
     for c in range(CHUNKS + LAG):
         if c < CHUNKS:
             primal = first_primal(c, primal)
+        if c == CHUNKS - 1:
+            for k in range(CHUNKS // 2, CHUNKS):
+                send_start(k)
         if c >= LAG:
             dual = first_dual(c - LAG, dual)
 
@@ -225,11 +240,6 @@
     c = CHUNKS - 1
     y1_cp[c] = send_prices(y1, yb1, yo1, y1_ss, y1_rs, c)
 
-    f1_cp = []
-    for c in range(CHUNKS):
-        mix_arrivals([s1[t, span(c), :] for t in range(ROWS)], fs_1, c)
-        f1_cp.append(send_arrivals(fs_1, v1.at[3:4, span(c)], fb_1, fh_1, f1_ss, f1_rs, c))
-
     for cp in r1_cp:
         cp.wait_recv()
     mine = jnp.sum(rows1[...], axis=0)
@@ -273,13 +283,6 @@
         m_cp.append(
             send(m_send.at[span(c)], m_recv.at[span(c)], m_ss.at[c], m_rs.at[c], there(0, 1))
         )
-    outs = [
-        pltpu.make_async_copy(v2, stock_out, out_sem.at[0]),
-        pltpu.make_async_copy(s2, ship_out, out_sem.at[1]),
-    ]
-    for cp in outs:
-        cp.start()
-
     f2_cp = []
 
     def last_arrivals(c):
@@ -307,11 +310,11 @@
         for cp in f1_cp[c]:
             cp.wait_recv()
         _, receipts = arrivals(fb_1, c)
-        v_rows = [v1[t, span(c), :] for t in range(ROWS)]
-        s_rows = [s1[t, span(c), :] for t in range(ROWS)]
+        v_rows = [v0[t, span(c), :] for t in range(ROWS)]
+        s_rows = [s0[t, span(c), :] for t in range(ROWS)]
         rows = balance_of(v_rows, s_rows, fh_1, receipts, c)
         for t in range(ROWS):
-            bal1[t, span(c), :] = rows[t]
+            bal1[t, span(c), :] = 0.5 * (bal1[t, span(c), :] + rows[t])
 
     for cp in p1_cp:
         cp.wait_recv()
@@ -342,18 +345,22 @@
             )
             flow = flow + (receipts[t] - s_rows[t] - wanted)
             pj[t, span(c), :] = flow
-    outs.append(pltpu.make_async_copy(y2, dual_out, out_sem.at[2]))
-    outs[-1].start()
-
     for cp in p2_cp:
         cp.wait_recv()
-    for t in range(ROWS):
-        pj[t] = pj[t] + pref[...]
-    outs.append(pltpu.make_async_copy(pj, proj_out, out_sem.at[3]))
-    outs[-1].start()
     for cp in sends:
         cp.wait_send()
-    for cp in outs:
+
+
+def finish(v2, s2, y2, pj, pref, stock_out, ship_out, dual_out, proj_out, total, sem):
+    copies = []
+    for k, (src, dst) in enumerate(((v2, stock_out), (s2, ship_out), (y2, dual_out))):
+        copies.append(pltpu.make_async_copy(src, dst, sem.at[k]))
+        copies[-1].start()
+    for t in range(ROWS):
+        total[t] = pj[t] + pref[...]
+        copies.append(pltpu.make_async_copy(total.at[t], proj_out.at[t], sem.at[3 + t]))
+        copies[-1].start()
+    for cp in copies:
         cp.wait()
 
 
@@ -361,8 +368,11 @@
     items = stock.shape[-1]
     panels = items // PANEL
 
+    def in_hbm(a, *shape):
+        return pltpu.with_memory_space_constraint(a.reshape(shape), pltpu.HBM)
+
     def view(a):
-        return a.reshape(ROWS, panels, PANEL)
+        return in_hbm(a, ROWS, panels, PANEL)
 
     slab = (ROWS, panels, PANEL)
 
@@ -377,30 +387,30 @@
         [vmem(*slab)] * 6
         + [vmem(*slab, dtype=jnp.int32), vmem(panels, PANEL, dtype=jnp.int32), vmem(PANEL, PANEL)]
         + [vmem(2 * PANEL, 2 * PANEL, dtype=BF16)] * 2
-        + [vmem(*slab)] * 8
+        + [vmem(*slab)] * 4
         + [vmem(5, panels, PANEL), vmem(1, panels, PANEL)] * 2
         + [vmem(5, panels, PANEL), vmem(1, panels, PANEL)] * 2
         + exchange
         + exchange
         + [vmem(panels, PANEL)] * 4
         + [vmem(weeks, panels // weeks, PANEL)] * 2
-        + [vmem(panels, PANEL)]
         + [vmem(1, PANEL), vmem(weeks, 1, PANEL), vmem(1, PANEL), vmem(regions, 1, PANEL)]
-        + [pltpu.SemaphoreType.DMA((9,)), pltpu.SemaphoreType.DMA((4,))]
+        + [pltpu.SemaphoreType.DMA((9,))]
         + sems(3 * CHUNKS) * 5
         + sems(CHUNKS)
         + sems(weeks)
         + sems(regions)
         + sems(weeks) * 2
     )
-    outs = pl.pallas_call(
+    parts = pl.pallas_call(
         functools.partial(kernel, weeks, regions, panels),
-        out_shape=[jax.ShapeDtypeStruct(slab, F32)] * 4,
-        in_specs=[pl.BlockSpec(memory_space=pl.ANY)] * 9,
-        out_specs=[pl.BlockSpec(memory_space=pl.ANY)] * 4,
+        out_shape=[jax.ShapeDtypeStruct(slab, F32)] * 4
+        + [jax.ShapeDtypeStruct((panels, PANEL), F32)],
+        in_specs=[pl.BlockSpec(memory_space=pltpu.HBM)] * 9,
+        out_specs=[pl.BlockSpec(memory_space=pltpu.VMEM)] * 5,
         scratch_shapes=scratch,
         compiler_params=pltpu.CompilerParams(
-            collective_id=0, has_side_effects=True, vmem_limit_bytes=48 * 1024 * 1024
+            collective_id=0, has_side_effects=True, vmem_limit_bytes=40 * 1024 * 1024
         ),
         cost_estimate=pl.CostEstimate(
             flops=2 * 6 * 5 * 5 * panels * PANEL * PANEL,
@@ -410,8 +420,17 @@
         name="primal_dual",
     )(
         view(stock), view(ship), view(dual), view(demand), view(hold), view(cost), view(cap),
-        lead.reshape(panels, PANEL), mix.reshape(PANEL, PANEL),
+        in_hbm(lead, panels, PANEL), in_hbm(mix, PANEL, PANEL),
     )
+    outs = pl.pallas_call(
+        finish,
+        out_shape=[jax.ShapeDtypeStruct(slab, F32)] * 4,
+        in_specs=[pl.BlockSpec(memory_space=pltpu.VMEM)] * 5,
+        out_specs=[pl.BlockSpec(memory_space=pltpu.HBM)] * 4,
+        scratch_shapes=[vmem(*slab), pltpu.SemaphoreType.DMA((3 + ROWS,))],
+        compiler_params=pltpu.CompilerParams(vmem_limit_bytes=8 * 1024 * 1024),
+        name="finish",
+    )(*parts)
     return tuple(o.reshape(ROWS, 1, items) for o in outs)
 
 

time: 78.5 us -> 66.7 us (0.85)
  local copies, waits for them, and re-layouts: 12.2 us -> 0 us
    unnamed x22 -> x0, local copies, waits for them, and re-layouts: 12.2 us -> none
    pallas_call x0 -> x1, Pallas kernels: none -> 1.37 us  [shards(): pl.pallas_call(finish, out_shape=[jax.ShapeDtypeStruct(slab, F32)] * 4, i...]
where the time goes in v2:
time: 66.7 us; the launch traced here: 66.5 us
  Pallas kernels  65.9 us (99%)
    pallas_call x1, Pallas kernels, shards(): pl.pallas_call(functools.partial(kernel, weeks, regions, panels), out_sha...  64.5 us
    pallas_call x1, Pallas kernels, shards(): pl.pallas_call(finish, out_shape=[jax.ShapeDtypeStruct(slab, F32)] * 4, i...  1.37 us

profile of v2, /device:TPU:2, one launch (start us, length us, event | category | flops | bytes accessed | tf_op | source)
XLA Modules:
  0.0 66.5 jit_solution(13205107773508943779)
XLA Ops:
  0.6 64.5 %primal_dual.1 = (f32[4,256,128]{2,1,0:T(8,128)S(1)}, f32[4,256,128]{2,1,0:T(8,128)S(1)}, f32[4,256,128]{2,1,0:T(8,128)S(1)}, f32[4,256,128]{2,1,0:T(8,128)S(1)}, f32[256,128]{1,0:T(8,128)S(1)}) custom-call(f32[4,256,128]{2,1,0:T(8,128)} %bitcast.13, f32[4,256,128]{2,1,0:T(8,128)} %bitcast.14, f32[4,256,128]{2,1,0:T(8,128)} %bitcast.15, ...), custom_call_target="tpu_custom_call" | custom-call | flops 1258291200 | bytes 6291456 | tf_op jit(solution)/shard_map/primal_dual/pallas_call | solution.py:405
  65.2 1.4 %finish.1 = (f32[4,256,128]{2,1,0:T(8,128)}, f32[4,256,128]{2,1,0:T(8,128)}, f32[4,256,128]{2,1,0:T(8,128)}, f32[4,256,128]{2,1,0:T(8,128)}) custom-call(f32[4,256,128]{2,1,0:T(8,128)S(1)} %get-tuple-element.13.v2, f32[4,256,128]{2,1,0:T(8,128)S(1)} %get-tuple-element.14.s2, f32[4,256,128]{2,1,0:T(8,128)S(1)} %get-tuple-element.15.y2, ...), custom_call_target="tpu_custom_call" | custom-call | tf_op jit(solution)/shard_map/finish/pallas_call | solution.py:425

commit v3 on v2

--- a/solution.py
+++ b/solution.py
@@ -9,7 +9,8 @@
 
 PANEL = 128
 ROWS = 4
-CHUNKS = 4
+SHARES = (8, 8, 7, 6, 3)
+CHUNKS = len(SHARES)
 LAG = 2
 STEP_ETA = 0.25
 EPS_MOVE = 1e-06
@@ -36,21 +37,21 @@
         v0, s0, y0, dem, ch, cs, cap, lead, mixw,
         w_fwd, w_adj,
         v1, s1, y1, bal1,
-        yb0, yo0, yb1, yo1,
-        fs_t, fv_t, fb_t, fh_t,
-        fs_1, fb_1, fh_1,
-        fs_2, fb_2, fh_2,
+        yb0, yb1,
+        fs_t, fv_t, fb_t,
+        fs_1, fb_1,
+        fs_2, fb_2,
         m_send, m_recv, s_sum, net, a1, a2,
         row1, rows1, row2, rows2,
-        load_sem,
-        y0_ss, y0_rs, y1_ss, y1_rs, ft_ss, ft_rs, f1_ss, f1_rs, f2_ss, f2_rs,
-        m_ss, m_rs, r1_ss, r1_rs, r2_ss, r2_rs, p1_ss, p1_rs, p2_ss, p2_rs,
+        load_sem, send_sem, wide_sem,
+        y0_rs, y1_rs, ft_rs, f1_rs, f2_rs, m_rs,
     ) = refs
     w = lax.axis_index("week")
     r = lax.axis_index("region")
     first = w == 0
     last = w == weeks - 1
-    size = panels // CHUNKS
+    sizes = [panels * k // sum(SHARES) for k in SHARES]
+    starts = [sum(sizes[:c]) for c in range(CHUNKS)]
     piece = panels // weeks
 
     def there(dw, dr):
@@ -74,34 +75,28 @@
     barrier = pltpu.get_barrier_semaphore()
     for dw, dr in partners:
         pl.semaphore_signal(barrier, inc=1, device_id=there(dw, dr), device_id_type=MESH)
-    sends = []
-
     def send(src, dst, ss, rs, to):
-        cp = pltpu.make_async_remote_copy(
+        pltpu.make_async_remote_copy(
             src_ref=src, dst_ref=dst, send_sem=ss, recv_sem=rs, device_id=to, device_id_type=MESH
-        )
-        cp.start()
-        sends.append(cp)
-        return cp
+        ).start()
+
+    def wait_for(ref, sem):
+        pltpu.make_async_copy(ref, ref, sem).wait()
 
     def span(c):
-        return pl.ds(c * size, size)
-
-    def send_prices(y, yb, yo, ss, rs, c):
-        k = 3 * c
-        return [
-            send(y.at[0:2, span(c)], yb.at[3:5, span(c)], ss.at[k], rs.at[k], there(-1, -1)),
-            send(y.at[0:1, span(c)], yo.at[:, span(c)], ss.at[k + 1], rs.at[k + 1], there(-1, 0)),
-            send(y.at[1:4, span(c)], yb.at[0:3, span(c)], ss.at[k + 2], rs.at[k + 2], there(0, -1)),
-        ]
-
-    def send_arrivals(fs, fv, fb, fh, ss, rs, c):
-        k = 3 * c
-        return [
-            send(fs.at[3:5, span(c)], fb.at[3:5, span(c)], ss.at[k], rs.at[k], there(1, 1)),
-            send(fv, fh.at[:, span(c)], ss.at[k + 1], rs.at[k + 1], there(1, 0)),
-            send(fs.at[0:3, span(c)], fb.at[0:3, span(c)], ss.at[k + 2], rs.at[k + 2], there(0, 1)),
-        ]
+        return pl.ds(starts[c], sizes[c])
+
+    def send_prices(y, yb, ss, rs, c):
+        at = span(c)
+        send(y.at[0:2, at], yb.at[3:5, at], ss, rs.at[c], there(-1, -1))
+        send(y.at[0:1, at], yb.at[5:6, at], ss, rs.at[c], there(-1, 0))
+        send(y.at[1:4, at], yb.at[0:3, at], ss, rs.at[c], there(0, -1))
+
+    def send_arrivals(fs, fv, fb, ss, rs, c):
+        at = span(c)
+        send(fs.at[3:5, at], fb.at[3:5, at], ss, rs.at[c], there(1, 1))
+        send(fv, fb.at[5:6, at], ss, rs.at[c], there(1, 0))
+        send(fs.at[0:3, at], fb.at[0:3, at], ss, rs.at[c], there(0, 1))
 
     def mix(values, weight):
         hi = values.astype(BF16)
@@ -109,14 +104,15 @@
         both = jnp.dot(jnp.concatenate([hi, lo], axis=1), weight[...], preferred_element_type=F32)
         return both[:, :PANEL] + both[:, PANEL:]
 
-    def pulled_gradients(y, yb, yo, c):
-        pulled = mix(yb[:, span(c), :].reshape(5 * size, PANEL), w_adj).reshape(5, size, PANEL)
+    def pulled_gradients(y, yb, c):
+        pulled = mix(yb[0:5, span(c), :].reshape(5 * sizes[c], PANEL), w_adj)
+        pulled = pulled.reshape(5, sizes[c], PANEL)
         pulled = [pulled[k] for k in range(5)]
         pulled[3] = jnp.where(last, 0.0, pulled[3])
         pulled[4] = jnp.where(last, 0.0, pulled[4])
         short = lead[span(c), :] == 1
         rows = [y[t, span(c), :] for t in range(ROWS)]
-        after = rows[1:] + [jnp.where(last, 0.0, yo[0, span(c), :])]
+        after = rows[1:] + [jnp.where(last, 0.0, yb[5, span(c), :])]
         grad_v = [rows[t] - after[t] for t in range(ROWS)]
         grad_s = [rows[t] - jnp.where(short, pulled[t], pulled[t + 1]) for t in range(ROWS)]
         return grad_v, grad_s
@@ -133,19 +129,19 @@
             ],
             axis=0,
         )
-        fs[:, span(c), :] = mix(lagged, w_fwd).reshape(5, size, PANEL)
+        fs[:, span(c), :] = mix(lagged, w_fwd).reshape(5, sizes[c], PANEL)
 
     def arrivals(fb, c):
         early = [jnp.where(first, 0.0, fb[3 + k, span(c), :]) for k in range(2)]
         own = [fb[k, span(c), :] for k in range(3)]
         return early, [early[0], own[0] + early[1], own[1], own[2]]
 
-    def balance_of(v_rows, s_rows, fh, receipts, c):
-        before = [jnp.where(first, 0.0, fh[0, span(c), :])] + v_rows[:-1]
+    def balance_of(v_rows, s_rows, fb, receipts, c):
+        before = [jnp.where(first, 0.0, fb[5, span(c), :])] + v_rows[:-1]
         return [v_rows[t] - before[t] + s_rows[t] - receipts[t] for t in range(ROWS)]
 
     def fold(values):
-        return jnp.sum(values.reshape(size // 8, 8, PANEL), axis=0)
+        return jnp.sum(values.reshape(values.shape[0] // 8, 8, PANEL), axis=0)
 
     loads[1].wait()
     for weight, dest in ((mixw[...], w_fwd), (mixw[...].T, w_adj)):
@@ -153,7 +149,6 @@
         lo = (weight - hi.astype(F32)).astype(BF16)
         half = jnp.concatenate([hi, lo], axis=1)
         dest[...] = jnp.concatenate([half, half], axis=0)
-    f1_cp = {}
     for cp in loads[2:5]:
         cp.wait()
     for c in range(CHUNKS):
@@ -161,11 +156,12 @@
     loads[0].wait()
 
     def send_start(c):
-        f1_cp[c] = send_arrivals(fs_1, v0.at[3:4, span(c)], fb_1, fh_1, f1_ss, f1_rs, c)
+        send_arrivals(fs_1, v0.at[3:4, span(c)], fb_1, send_sem.at[0], f1_rs, c)
 
     pl.semaphore_wait(barrier, len(partners))
 
-    y0_cp = [send_prices(y0, yb0, yo0, y0_ss, y0_rs, c) for c in range(CHUNKS)]
+    for c in range(CHUNKS):
+        send_prices(y0, yb0, send_sem.at[1], y0_rs, c)
     for c in range(CHUNKS // 2):
         send_start(c)
     for cp in loads[5:]:
@@ -173,13 +169,10 @@
 
     primal = jnp.zeros((8, PANEL), F32)
     dual = jnp.zeros((8, PANEL), F32)
-    ft_cp = {}
-    y1_cp = {}
 
     def first_primal(c, primal):
-        for cp in y0_cp[c]:
-            cp.wait_recv()
-        grad_v, grad_s = pulled_gradients(y0, yb0, yo0, c)
+        wait_for(yb0.at[:, span(c)], y0_rs.at[c])
+        grad_v, grad_s = pulled_gradients(y0, yb0, c)
         ahead = []
         for t in range(ROWS):
             old_v = v0[t, span(c), :]
@@ -196,16 +189,15 @@
             primal = primal + fold((new_v - old_v) ** 2) + fold((new_s - old_s) ** 2)
             ahead.append(2.0 * new_s - old_s)
         mix_arrivals(ahead, fs_t, c)
-        ft_cp[c] = send_arrivals(fs_t, fv_t.at[:, span(c)], fb_t, fh_t, ft_ss, ft_rs, c)
+        send_arrivals(fs_t, fv_t.at[:, span(c)], fb_t, send_sem.at[2], ft_rs, c)
         return primal
 
     def first_dual(c, dual):
-        for cp in ft_cp[c]:
-            cp.wait_recv()
+        wait_for(fb_t.at[:, span(c)], ft_rs.at[c])
         _, receipts = arrivals(fb_t, c)
         v_rows = [2.0 * v1[t, span(c), :] - v0[t, span(c), :] for t in range(ROWS)]
         s_rows = [2.0 * s1[t, span(c), :] - s0[t, span(c), :] for t in range(ROWS)]
-        ahead = balance_of(v_rows, s_rows, fh_t, receipts, c)
+        ahead = balance_of(v_rows, s_rows, fb_t, receipts, c)
         for t in range(ROWS):
             bal1[t, span(c), :] = ahead[t]
             moved = STEP_ETA * (dem[t, span(c), :] - ahead[t])
@@ -213,7 +205,7 @@
             y1[t, span(c), :] = new_y
             dual = dual + fold((new_y - y0[t, span(c), :]) ** 2)
         if c < CHUNKS - 1:
-            y1_cp[c] = send_prices(y1, yb1, yo1, y1_ss, y1_rs, c)
+            send_prices(y1, yb1, send_sem.at[3], y1_rs, c)
         return dual
 
     for c in range(CHUNKS + LAG):
@@ -233,32 +225,26 @@
         lane < half, primal + pltpu.roll(primal, half, 1), dual + pltpu.roll(dual, half, 1)
     )
     row1[...] = mine
-    r1_cp = [
-        send(row1, rows1.at[w], r1_ss.at[d], r1_rs.at[d], there(d, 0)) for d in w_off
-    ]
+    for d in w_off:
+        send(row1, rows1.at[w], wide_sem.at[0], wide_sem.at[1], there(d, 0))
     rows1[w] = mine
-    c = CHUNKS - 1
-    y1_cp[c] = send_prices(y1, yb1, yo1, y1_ss, y1_rs, c)
-
-    for cp in r1_cp:
-        cp.wait_recv()
+    send_prices(y1, yb1, send_sem.at[3], y1_rs, CHUNKS - 1)
+
+    wait_for(rows1.at[0 : weeks - 1], wide_sem.at[1])
     mine = jnp.sum(rows1[...], axis=0)
     row2[...] = mine
-    r2_cp = [
-        send(row2, rows2.at[r], r2_ss.at[d], r2_rs.at[d], there(0, d)) for d in range(1, regions)
-    ]
+    for d in range(1, regions):
+        send(row2, rows2.at[r], wide_sem.at[2], wide_sem.at[3], there(0, d))
     rows2[r] = mine
 
     for c in range(CHUNKS):
-        for cp in y1_cp[c]:
-            cp.wait_recv()
-        grad_v, grad_s = pulled_gradients(y1, yb1, yo1, c)
+        wait_for(yb1.at[:, span(c)], y1_rs.at[c])
+        grad_v, grad_s = pulled_gradients(y1, yb1, c)
         for t in range(ROWS):
             ch[t, span(c), :] = ch[t, span(c), :] - grad_v[t]
             cs[t, span(c), :] = cs[t, span(c), :] - grad_s[t]
 
-    for cp in r2_cp:
-        cp.wait_recv()
+    wait_for(rows2.at[0 : regions - 1], wide_sem.at[3])
     total = jnp.sum(rows2[...], axis=0)
     moved_primal = jnp.sum(jnp.where(lane < half, total, 0.0), axis=1, keepdims=True)
     moved_dual = jnp.sum(jnp.where(lane < half, 0.0, total), axis=1, keepdims=True)
@@ -267,9 +253,8 @@
     primal_step = STEP_ETA / weight
     dual_step = STEP_ETA * weight
 
-    m_cp = []
-    for c in range(CHUNKS):
-        sums = jnp.zeros((size, PANEL), F32)
+    for c in range(CHUNKS):
+        sums = jnp.zeros((sizes[c], PANEL), F32)
         for t in range(ROWS):
             v2[t, span(c), :] = jnp.maximum(v1[t, span(c), :] - primal_step * ch[t, span(c), :], 0.0)
             new_s = jnp.minimum(
@@ -280,63 +265,47 @@
             sums = sums + new_s
         s_sum[span(c), :] = sums
         m_send[span(c), :] = mix(sums, w_fwd)
-        m_cp.append(
-            send(m_send.at[span(c)], m_recv.at[span(c)], m_ss.at[c], m_rs.at[c], there(0, 1))
-        )
-    f2_cp = []
-
-    def last_arrivals(c):
-        mix_arrivals([s2[t, span(c), :] for t in range(ROWS)], fs_2, c)
-        f2_cp.append(send_arrivals(fs_2, v2.at[3:4, span(c)], fb_2, fh_2, f2_ss, f2_rs, c))
-
-    for c in range(CHUNKS):
-        last_arrivals(c)
-
-    for c in range(CHUNKS):
-        m_cp[c].wait_recv()
+        send(m_send.at[span(c)], m_recv.at[span(c)], wide_sem.at[4], m_rs.at[c], there(0, 1))
+    for c in range(CHUNKS):
+        wait_for(m_recv.at[span(c)], m_rs.at[c])
         sums = m_recv[span(c), :] - s_sum[span(c), :]
         for t in range(ROWS):
             sums = sums - dem[t, span(c), :]
         net[span(c), :] = sums
-    p1_cp = []
     for d in w_off:
         to = there(d, 0)
-        p1_cp.append(
-            send(net.at[pl.ds(to[0] * piece, piece)], a1.at[w], p1_ss.at[d], p1_rs.at[d], to)
-        )
+        send(net.at[pl.ds(to[0] * piece, piece)], a1.at[w], wide_sem.at[5], wide_sem.at[6], to)
     a1[w] = net[pl.ds(w * piece, piece), :]
 
     for c in range(CHUNKS):
-        for cp in f1_cp[c]:
-            cp.wait_recv()
+        mix_arrivals([s2[t, span(c), :] for t in range(ROWS)], fs_2, c)
+        send_arrivals(fs_2, v2.at[3:4, span(c)], fb_2, send_sem.at[4], f2_rs, c)
+
+    for c in range(CHUNKS):
+        wait_for(fb_1.at[:, span(c)], f1_rs.at[c])
         _, receipts = arrivals(fb_1, c)
         v_rows = [v0[t, span(c), :] for t in range(ROWS)]
         s_rows = [s0[t, span(c), :] for t in range(ROWS)]
-        rows = balance_of(v_rows, s_rows, fh_1, receipts, c)
+        rows = balance_of(v_rows, s_rows, fb_1, receipts, c)
         for t in range(ROWS):
             bal1[t, span(c), :] = 0.5 * (bal1[t, span(c), :] + rows[t])
 
-    for cp in p1_cp:
-        cp.wait_recv()
+    wait_for(a1.at[0 : weeks - 1], wide_sem.at[6])
     running = jnp.zeros((piece, PANEL), F32)
     for k in range(weeks):
         a2[k] = running
         running = running + a1[k]
-    p2_cp = []
     for d in w_off:
         to = there(d, 0)
-        p2_cp.append(
-            send(a2.at[to[0]], pref.at[pl.ds(w * piece, piece)], p2_ss.at[d], p2_rs.at[d], to)
-        )
+        send(a2.at[to[0]], pref.at[pl.ds(w * piece, piece)], wide_sem.at[7], wide_sem.at[8], to)
     pref[pl.ds(w * piece, piece), :] = a2[w]
 
     for c in range(CHUNKS):
-        for cp in f2_cp[c]:
-            cp.wait_recv()
+        wait_for(fb_2.at[:, span(c)], f2_rs.at[c])
         early, receipts = arrivals(fb_2, c)
         v_rows = [v2[t, span(c), :] for t in range(ROWS)]
         s_rows = [s2[t, span(c), :] for t in range(ROWS)]
-        rows = balance_of(v_rows, s_rows, fh_2, receipts, c)
+        rows = balance_of(v_rows, s_rows, fb_2, receipts, c)
         flow = -early[0] - early[1]
         for t in range(ROWS):
             wanted = dem[t, span(c), :]
@@ -345,10 +314,14 @@
             )
             flow = flow + (receipts[t] - s_rows[t] - wanted)
             pj[t, span(c), :] = flow
-    for cp in p2_cp:
-        cp.wait_recv()
-    for cp in sends:
-        cp.wait_send()
+    for k, landing in enumerate((fb_1, yb0, fb_t, yb1, fb_2)):
+        wait_for(landing, send_sem.at[k])
+    wait_for(rows1.at[0 : weeks - 1], wide_sem.at[0])
+    wait_for(rows2.at[0 : regions - 1], wide_sem.at[2])
+    wait_for(m_recv, wide_sem.at[4])
+    wait_for(a1.at[0 : weeks - 1], wide_sem.at[5])
+    wait_for(a2.at[0 : weeks - 1], wide_sem.at[7])
+    wait_for(pref.at[0 : panels - piece], wide_sem.at[8])
 
 
 def finish(v2, s2, y2, pj, pref, stock_out, ship_out, dual_out, proj_out, total, sem):
@@ -380,27 +353,21 @@
         return pltpu.VMEM(shape, dtype)
 
     def sems(n):
-        return [pltpu.SemaphoreType.DMA((n,))] * 2
-
-    exchange = [vmem(5, panels, PANEL), vmem(5, panels, PANEL), vmem(1, panels, PANEL)]
+        return pltpu.SemaphoreType.DMA((n,))
+
     scratch = (
         [vmem(*slab)] * 6
         + [vmem(*slab, dtype=jnp.int32), vmem(panels, PANEL, dtype=jnp.int32), vmem(PANEL, PANEL)]
         + [vmem(2 * PANEL, 2 * PANEL, dtype=BF16)] * 2
         + [vmem(*slab)] * 4
-        + [vmem(5, panels, PANEL), vmem(1, panels, PANEL)] * 2
-        + [vmem(5, panels, PANEL), vmem(1, panels, PANEL)] * 2
-        + exchange
-        + exchange
+        + [vmem(6, panels, PANEL)] * 2
+        + [vmem(5, panels, PANEL), vmem(1, panels, PANEL), vmem(6, panels, PANEL)]
+        + [vmem(5, panels, PANEL), vmem(6, panels, PANEL)] * 2
         + [vmem(panels, PANEL)] * 4
         + [vmem(weeks, panels // weeks, PANEL)] * 2
         + [vmem(1, PANEL), vmem(weeks, 1, PANEL), vmem(1, PANEL), vmem(regions, 1, PANEL)]
-        + [pltpu.SemaphoreType.DMA((9,))]
-        + sems(3 * CHUNKS) * 5
-        + sems(CHUNKS)
-        + sems(weeks)
-        + sems(regions)
-        + sems(weeks) * 2
+        + [sems(9), sems(5), sems(9)]
+        + [sems(CHUNKS)] * 6
     )
     parts = pl.pallas_call(
         functools.partial(kernel, weeks, regions, panels),

time: 66.7 us -> 62.2 us (0.933)
  Pallas kernels: 65.9 us -> 61.5 us
    pallas_call x1, Pallas kernels: 64.5 us -> 60.1 us  [shards(): pl.pallas_call(functools.partial(kernel, weeks, regions, panels), out_sha...]
where the time goes in v3:
time: 62.2 us; the launch traced here: 62.1 us
  Pallas kernels  61.5 us (99%)
  between operations  0.64 us (1%)
    pallas_call x1, Pallas kernels, shards(): pl.pallas_call(functools.partial(kernel, weeks, regions, panels), out_sha...  60.1 us
    pallas_call x1, Pallas kernels, shards(): pl.pallas_call(finish, out_shape=[jax.ShapeDtypeStruct(slab, F32)] * 4, i...  1.37 us

profile of v3, /device:TPU:2, one launch (start us, length us, event | category | flops | bytes accessed | tf_op | source)
XLA Modules:
  0.0 62.1 jit_solution(3712167267939006854)
XLA Ops:
  0.6 60.1 %primal_dual.1 = (f32[4,256,128]{2,1,0:T(8,128)S(1)}, f32[4,256,128]{2,1,0:T(8,128)S(1)}, f32[4,256,128]{2,1,0:T(8,128)S(1)}, f32[4,256,128]{2,1,0:T(8,128)S(1)}, f32[256,128]{1,0:T(8,128)S(1)}) custom-call(f32[4,256,128]{2,1,0:T(8,128)} %bitcast.13, f32[4,256,128]{2,1,0:T(8,128)} %bitcast.14, f32[4,256,128]{2,1,0:T(8,128)} %bitcast.15, ...), custom_call_target="tpu_custom_call" | custom-call | flops 1258291200 | bytes 6291456 | tf_op jit(solution)/shard_map/primal_dual/pallas_call | solution.py:372
  60.8 1.4 %finish.1 = (f32[4,256,128]{2,1,0:T(8,128)}, f32[4,256,128]{2,1,0:T(8,128)}, f32[4,256,128]{2,1,0:T(8,128)}, f32[4,256,128]{2,1,0:T(8,128)}) custom-call(f32[4,256,128]{2,1,0:T(8,128)S(1)} %get-tuple-element.13.v2, f32[4,256,128]{2,1,0:T(8,128)S(1)} %get-tuple-element.14.s2, f32[4,256,128]{2,1,0:T(8,128)S(1)} %get-tuple-element.15.y2, ...), custom_call_target="tpu_custom_call" | custom-call | tf_op jit(solution)/shard_map/finish/pallas_call | solution.py:392

commit v4 on v3

--- a/solution.py
+++ b/solution.py
@@ -11,6 +11,8 @@
 ROWS = 4
 SHARES = (8, 8, 7, 6, 3)
 CHUNKS = len(SHARES)
+EARLY = 2
+QUARTERS = (2, 1, 3, 0)
 LAG = 2
 STEP_ETA = 0.25
 EPS_MOVE = 1e-06
@@ -244,6 +246,8 @@
             ch[t, span(c), :] = ch[t, span(c), :] - grad_v[t]
             cs[t, span(c), :] = cs[t, span(c), :] - grad_s[t]
 
+    s_sum[...] = dem[0] + dem[1] + dem[2] + dem[3]
+
     wait_for(rows2.at[0 : regions - 1], wide_sem.at[3])
     total = jnp.sum(rows2[...], axis=0)
     moved_primal = jnp.sum(jnp.where(lane < half, total, 0.0), axis=1, keepdims=True)
@@ -253,33 +257,46 @@
     primal_step = STEP_ETA / weight
     dual_step = STEP_ETA * weight
 
-    for c in range(CHUNKS):
-        sums = jnp.zeros((sizes[c], PANEL), F32)
+    owners = weeks // 4
+    quarter = panels // 4
+
+    def quarter_at(k):
+        q = lax.rem(lax.div(w, owners) + k, 4)
+        return q, pl.ds(pl.multiple_of(q * quarter, 8), quarter)
+
+    for k in QUARTERS:
+        _, at = quarter_at(k)
+        sums = jnp.zeros((quarter, PANEL), F32)
+        for t in range(ROWS):
+            new_s = jnp.minimum(
+                jnp.maximum(s1[t, at, :] - primal_step * cs[t, at, :], 0.0), cap[t, at, :].astype(F32)
+            )
+            s2[t, at, :] = new_s
+            sums = sums + new_s
+        s_sum[at, :] = s_sum[at, :] + sums
+        m_send[at, :] = mix(sums, w_fwd)
+        send(m_send.at[at], m_recv.at[at], wide_sem.at[4], m_rs.at[k], there(0, 1))
+
+    def last_arrivals(c):
         for t in range(ROWS):
             v2[t, span(c), :] = jnp.maximum(v1[t, span(c), :] - primal_step * ch[t, span(c), :], 0.0)
-            new_s = jnp.minimum(
-                jnp.maximum(s1[t, span(c), :] - primal_step * cs[t, span(c), :], 0.0),
-                cap[t, span(c), :].astype(F32),
-            )
-            s2[t, span(c), :] = new_s
-            sums = sums + new_s
-        s_sum[span(c), :] = sums
-        m_send[span(c), :] = mix(sums, w_fwd)
-        send(m_send.at[span(c)], m_recv.at[span(c)], wide_sem.at[4], m_rs.at[c], there(0, 1))
-    for c in range(CHUNKS):
-        wait_for(m_recv.at[span(c)], m_rs.at[c])
-        sums = m_recv[span(c), :] - s_sum[span(c), :]
-        for t in range(ROWS):
-            sums = sums - dem[t, span(c), :]
-        net[span(c), :] = sums
-    for d in w_off:
-        to = there(d, 0)
-        send(net.at[pl.ds(to[0] * piece, piece)], a1.at[w], wide_sem.at[5], wide_sem.at[6], to)
-    a1[w] = net[pl.ds(w * piece, piece), :]
-
-    for c in range(CHUNKS):
         mix_arrivals([s2[t, span(c), :] for t in range(ROWS)], fs_2, c)
         send_arrivals(fs_2, v2.at[3:4, span(c)], fb_2, send_sem.at[4], f2_rs, c)
+
+    for c in range(EARLY):
+        last_arrivals(c)
+
+    for k in QUARTERS:
+        q, at = quarter_at(k)
+        wait_for(m_recv.at[at], m_rs.at[k])
+        net[at, :] = m_recv[at, :] - s_sum[at, :]
+        for j in range(0 if k else 1, owners):
+            to = q * owners + lax.rem(w + j, owners)
+            send(net.at[pl.ds(to * piece, piece)], a1.at[w], wide_sem.at[5], wide_sem.at[6], (to, r))
+    a1[w] = net[pl.ds(w * piece, piece), :]
+
+    for c in range(EARLY, CHUNKS):
+        last_arrivals(c)
 
     for c in range(CHUNKS):
         wait_for(fb_1.at[:, span(c)], f1_rs.at[c])
@@ -367,7 +384,8 @@
         + [vmem(weeks, panels // weeks, PANEL)] * 2
         + [vmem(1, PANEL), vmem(weeks, 1, PANEL), vmem(1, PANEL), vmem(regions, 1, PANEL)]
         + [sems(9), sems(5), sems(9)]
-        + [sems(CHUNKS)] * 6
+        + [sems(CHUNKS)] * 5
+        + [sems(4)]
     )
     parts = pl.pallas_call(
         functools.partial(kernel, weeks, regions, panels),

time: 62.2 us -> 60.9 us (0.979)
  Pallas kernels: 61.5 us -> 60.1 us
    pallas_call x1, Pallas kernels: 60.1 us -> 58.8 us  [shards(): pl.pallas_call(functools.partial(kernel, weeks, regions, panels), out_sha...]
where the time goes in v4:
time: 60.9 us; the launch traced here: 60.8 us
  Pallas kernels  60.1 us (99%)
  between operations  0.64 us (1%)
    pallas_call x1, Pallas kernels, shards(): pl.pallas_call(functools.partial(kernel, weeks, regions, panels), out_sha...  58.8 us
    pallas_call x1, Pallas kernels, shards(): pl.pallas_call(finish, out_shape=[jax.ShapeDtypeStruct(slab, F32)] * 4, i...  1.37 us

profile of v4, /device:TPU:2, one launch (start us, length us, event | category | flops | bytes accessed | tf_op | source)
XLA Modules:
  0.0 60.8 jit_solution(23937916583573378)
XLA Ops:
  0.6 58.8 %primal_dual.1 = (f32[4,256,128]{2,1,0:T(8,128)S(1)}, f32[4,256,128]{2,1,0:T(8,128)S(1)}, f32[4,256,128]{2,1,0:T(8,128)S(1)}, f32[4,256,128]{2,1,0:T(8,128)S(1)}, f32[256,128]{1,0:T(8,128)S(1)}) custom-call(f32[4,256,128]{2,1,0:T(8,128)} %bitcast.13, f32[4,256,128]{2,1,0:T(8,128)} %bitcast.14, f32[4,256,128]{2,1,0:T(8,128)} %bitcast.15, ...), custom_call_target="tpu_custom_call" | custom-call | flops 1258291200 | bytes 6291456 | tf_op jit(solution)/shard_map/primal_dual/pallas_call | solution.py:390
  59.4 1.4 %finish.1 = (f32[4,256,128]{2,1,0:T(8,128)}, f32[4,256,128]{2,1,0:T(8,128)}, f32[4,256,128]{2,1,0:T(8,128)}, f32[4,256,128]{2,1,0:T(8,128)}) custom-call(f32[4,256,128]{2,1,0:T(8,128)S(1)} %get-tuple-element.13.v2, f32[4,256,128]{2,1,0:T(8,128)S(1)} %get-tuple-element.14.s2, f32[4,256,128]{2,1,0:T(8,128)S(1)} %get-tuple-element.15.y2, ...), custom_call_target="tpu_custom_call" | custom-call | tf_op jit(solution)/shard_map/finish/pallas_call | solution.py:410

commit v5 on v4

--- a/solution.py
+++ b/solution.py
@@ -45,7 +45,7 @@
         fs_2, fb_2,
         m_send, m_recv, s_sum, net, a1, a2,
         row1, rows1, row2, rows2,
-        load_sem, send_sem, wide_sem,
+        load_sem, send_sem, wide_sem, round_sem,
         y0_rs, y1_rs, ft_rs, f1_rs, f2_rs, m_rs,
     ) = refs
     w = lax.axis_index("week")
@@ -70,13 +70,30 @@
         cp.start()
         loads.append(cp)
 
+    def others(offsets):
+        pairs = dict.fromkeys((a % weeks, b % regions) for a, b in offsets)
+        return [p for p in pairs if p != (0, 0)]
+
+    def signal(sem, offsets):
+        for dw, dr in offsets:
+            pl.semaphore_signal(sem, inc=1, device_id=there(dw, dr), device_id_type=MESH)
+
     w_off = week_offsets(weeks)
-    near = [(0, 1), (1, 1), (1, 0), (0, -1), (-1, -1), (-1, 0)]
-    far = [(d, 0) for d in w_off] + [(0, d) for d in range(1, regions)]
-    partners = list(dict.fromkeys((a % weeks, b % regions) for a, b in near + far))
+    near = others([(0, 1), (0, -1), (1, 1), (-1, -1), (1, 0), (-1, 0), (4, 0), (-4, 0)])
+    rounds = [
+        others([(4, 0), (-4, 0), (0, 1), (0, -1)]),
+        others([(8, 0), (-8, 0), (0, 2), (0, -2)]),
+        others([(1, 0), (-1, 0)]),
+    ]
     barrier = pltpu.get_barrier_semaphore()
-    for dw, dr in partners:
-        pl.semaphore_signal(barrier, inc=1, device_id=there(dw, dr), device_id_type=MESH)
+    signal(barrier, near)
+
+    def spread(k):
+        if k > 0 and rounds[k - 1]:
+            pl.semaphore_wait(round_sem.at[k - 1], len(rounds[k - 1]))
+        if k < len(rounds):
+            signal(round_sem.at[k], rounds[k])
+
     def send(src, dst, ss, rs, to):
         pltpu.make_async_remote_copy(
             src_ref=src, dst_ref=dst, send_sem=ss, recv_sem=rs, device_id=to, device_id_type=MESH
@@ -145,6 +162,12 @@
     def fold(values):
         return jnp.sum(values.reshape(values.shape[0] // 8, 8, PANEL), axis=0)
 
+    loads[0].wait()
+    pl.semaphore_wait(barrier, len(near))
+    for c in range(CHUNKS):
+        send_prices(y0, yb0, send_sem.at[1], y0_rs, c)
+    spread(0)
+
     loads[1].wait()
     for weight, dest in ((mixw[...], w_fwd), (mixw[...].T, w_adj)):
         hi = weight.astype(BF16)
@@ -153,19 +176,14 @@
         dest[...] = jnp.concatenate([half, half], axis=0)
     for cp in loads[2:5]:
         cp.wait()
+
+    def send_start(c):
+        send_arrivals(fs_1, v0.at[3:4, span(c)], fb_1, send_sem.at[0], f1_rs, c)
+
     for c in range(CHUNKS):
         mix_arrivals([s0[t, span(c), :] for t in range(ROWS)], fs_1, c)
-    loads[0].wait()
-
-    def send_start(c):
-        send_arrivals(fs_1, v0.at[3:4, span(c)], fb_1, send_sem.at[0], f1_rs, c)
-
-    pl.semaphore_wait(barrier, len(partners))
-
-    for c in range(CHUNKS):
-        send_prices(y0, yb0, send_sem.at[1], y0_rs, c)
-    for c in range(CHUNKS // 2):
-        send_start(c)
+        if c < CHUNKS // 2:
+            send_start(c)
     for cp in loads[5:]:
         cp.wait()
 
@@ -218,6 +236,8 @@
                 send_start(k)
         if c >= LAG:
             dual = first_dual(c - LAG, dual)
+        if 0 < c <= len(rounds):
+            spread(c)
 
     lane = lax.broadcasted_iota(jnp.int32, (1, PANEL), 1)
     primal = jnp.sum(primal, axis=0, keepdims=True)
@@ -383,7 +403,7 @@
         + [vmem(panels, PANEL)] * 4
         + [vmem(weeks, panels // weeks, PANEL)] * 2
         + [vmem(1, PANEL), vmem(weeks, 1, PANEL), vmem(1, PANEL), vmem(regions, 1, PANEL)]
-        + [sems(9), sems(5), sems(9)]
+        + [sems(9), sems(5), sems(9), pltpu.SemaphoreType.REGULAR((3,))]
         + [sems(CHUNKS)] * 5
         + [sems(4)]
     )

time: 60.9 us -> 61.6 us (1.011)
  Pallas kernels: 60.1 us -> 60.9 us
    pallas_call x1, Pallas kernels: 58.8 us -> 59.6 us  [shards(): pl.pallas_call(functools.partial(kernel, weeks, regions, panels), out_sha...]
where the time goes in v5:
time: 61.6 us
  Pallas kernels  60.9 us (99%)
  between operations  0.64 us (1%)
    pallas_call x1, Pallas kernels, shards(): pl.pallas_call(functools.partial(kernel, weeks, regions, panels), out_sha...  59.6 us
    pallas_call x1, Pallas kernels, shards(): pl.pallas_call(finish, out_shape=[jax.ShapeDtypeStruct(slab, F32)] * 4, i...  1.37 us

profile of v5, /device:TPU:2, one launch (start us, length us, event | category | flops | bytes accessed | tf_op | source)
XLA Modules:
  0.0 61.6 jit_solution(18157256490773301188)
XLA Ops:
  0.6 59.6 %primal_dual.1 = (f32[4,256,128]{2,1,0:T(8,128)S(1)}, f32[4,256,128]{2,1,0:T(8,128)S(1)}, f32[4,256,128]{2,1,0:T(8,128)S(1)}, f32[4,256,128]{2,1,0:T(8,128)S(1)}, f32[256,128]{1,0:T(8,128)S(1)}) custom-call(f32[4,256,128]{2,1,0:T(8,128)} %bitcast.13, f32[4,256,128]{2,1,0:T(8,128)} %bitcast.14, f32[4,256,128]{2,1,0:T(8,128)} %bitcast.15, ...), custom_call_target="tpu_custom_call" | custom-call | flops 1258291200 | bytes 6291456 | tf_op jit(solution)/shard_map/primal_dual/pallas_call | solution.py:410
  60.2 1.4 %finish.1 = (f32[4,256,128]{2,1,0:T(8,128)}, f32[4,256,128]{2,1,0:T(8,128)}, f32[4,256,128]{2,1,0:T(8,128)}, f32[4,256,128]{2,1,0:T(8,128)}) custom-call(f32[4,256,128]{2,1,0:T(8,128)S(1)} %get-tuple-element.13.v2, f32[4,256,128]{2,1,0:T(8,128)S(1)} %get-tuple-element.14.s2, f32[4,256,128]{2,1,0:T(8,128)S(1)} %get-tuple-element.15.y2, ...), custom_call_target="tpu_custom_call" | custom-call | tf_op jit(solution)/shard_map/finish/pallas_call | solution.py:430

commit v6 on v5

--- a/solution.py
+++ b/solution.py
@@ -11,9 +11,10 @@
 ROWS = 4
 SHARES = (8, 8, 7, 6, 3)
 CHUNKS = len(SHARES)
-EARLY = 2
+EARLY = 1
+LATE = 2
 QUARTERS = (2, 1, 3, 0)
-LAG = 2
+LAG = 3
 STEP_ETA = 0.25
 EPS_MOVE = 1e-06
 MESH = pl.DeviceIdType.MESH
@@ -162,12 +163,6 @@
     def fold(values):
         return jnp.sum(values.reshape(values.shape[0] // 8, 8, PANEL), axis=0)
 
-    loads[0].wait()
-    pl.semaphore_wait(barrier, len(near))
-    for c in range(CHUNKS):
-        send_prices(y0, yb0, send_sem.at[1], y0_rs, c)
-    spread(0)
-
     loads[1].wait()
     for weight, dest in ((mixw[...], w_fwd), (mixw[...].T, w_adj)):
         hi = weight.astype(BF16)
@@ -182,8 +177,15 @@
 
     for c in range(CHUNKS):
         mix_arrivals([s0[t, span(c), :] for t in range(ROWS)], fs_1, c)
-        if c < CHUNKS // 2:
-            send_start(c)
+
+    loads[0].wait()
+    pl.semaphore_wait(barrier, len(near))
+    for c in range(CHUNKS):
+        send_prices(y0, yb0, send_sem.at[1], y0_rs, c)
+    spread(0)
+
+    for c in range(CHUNKS // 2):
+        send_start(c)
     for cp in loads[5:]:
         cp.wait()
 
@@ -315,7 +317,7 @@
             send(net.at[pl.ds(to * piece, piece)], a1.at[w], wide_sem.at[5], wide_sem.at[6], (to, r))
     a1[w] = net[pl.ds(w * piece, piece), :]
 
-    for c in range(EARLY, CHUNKS):
+    for c in range(EARLY, CHUNKS - LATE):
         last_arrivals(c)
 
     for c in range(CHUNKS):
@@ -336,6 +338,9 @@
         to = there(d, 0)
         send(a2.at[to[0]], pref.at[pl.ds(w * piece, piece)], wide_sem.at[7], wide_sem.at[8], to)
     pref[pl.ds(w * piece, piece), :] = a2[w]
+
+    for c in range(CHUNKS - LATE, CHUNKS):
+        last_arrivals(c)
 
     for c in range(CHUNKS):
         wait_for(fb_2.at[:, span(c)], f2_rs.at[c])

time: 61.6 us -> 60.2 us (0.977)
  the two profiles are of different devices: /device:TPU:2 before, /device:TPU:1 now
where the time goes in v6:
time: 60.2 us; the launch traced here: 60.1 us
  Pallas kernels  59.5 us (99%)
  between operations  0.64 us (1%)
    pallas_call x1, Pallas kernels, shards(): pl.pallas_call(functools.partial(kernel, weeks, regions, panels), out_sha...  58.1 us
    pallas_call x1, Pallas kernels, shards(): pl.pallas_call(finish, out_shape=[jax.ShapeDtypeStruct(slab, F32)] * 4, i...  1.37 us

profile of v6, /device:TPU:1, one launch (start us, length us, event | category | flops | bytes accessed | tf_op | source)
XLA Modules:
  0.0 60.1 jit_solution(6888520719956583776)
XLA Ops:
  0.6 58.1 %primal_dual.1 = (f32[4,256,128]{2,1,0:T(8,128)S(1)}, f32[4,256,128]{2,1,0:T(8,128)S(1)}, f32[4,256,128]{2,1,0:T(8,128)S(1)}, f32[4,256,128]{2,1,0:T(8,128)S(1)}, f32[256,128]{1,0:T(8,128)S(1)}) custom-call(f32[4,256,128]{2,1,0:T(8,128)} %bitcast.13, f32[4,256,128]{2,1,0:T(8,128)} %bitcast.14, f32[4,256,128]{2,1,0:T(8,128)} %bitcast.15, ...), custom_call_target="tpu_custom_call" | custom-call | flops 1258291200 | bytes 6291456 | tf_op jit(solution)/shard_map/primal_dual/pallas_call | solution.py:415
  58.7 1.4 %finish.1 = (f32[4,256,128]{2,1,0:T(8,128)}, f32[4,256,128]{2,1,0:T(8,128)}, f32[4,256,128]{2,1,0:T(8,128)}, f32[4,256,128]{2,1,0:T(8,128)}) custom-call(f32[4,256,128]{2,1,0:T(8,128)S(1)} %get-tuple-element.13.v2, f32[4,256,128]{2,1,0:T(8,128)S(1)} %get-tuple-element.14.s2, f32[4,256,128]{2,1,0:T(8,128)S(1)} %get-tuple-element.15.y2, ...), custom_call_target="tpu_custom_call" | custom-call | tf_op jit(solution)/shard_map/finish/pallas_call | solution.py:435

commit v7 on v6

--- a/solution.py
+++ b/solution.py
@@ -12,7 +12,7 @@
 SHARES = (8, 8, 7, 6, 3)
 CHUNKS = len(SHARES)
 EARLY = 1
-LATE = 2
+LATE = 1
 QUARTERS = (2, 1, 3, 0)
 LAG = 3
 STEP_ETA = 0.25

time: 60.2 us -> 59.4 us (0.987)
  the two profiles are of different devices: /device:TPU:1 before, /device:TPU:2 now
where the time goes in v7:
time: 59.4 us; the launch traced here: 59 us
  Pallas kernels  58.4 us (98%)
  between operations  0.64 us (1%)
    pallas_call x1, Pallas kernels, shards(): pl.pallas_call(functools.partial(kernel, weeks, regions, panels), out_sha...  57 us
    pallas_call x1, Pallas kernels, shards(): pl.pallas_call(finish, out_shape=[jax.ShapeDtypeStruct(slab, F32)] * 4, i...  1.37 us

profile of v7, /device:TPU:2, one launch (start us, length us, event | category | flops | bytes accessed | tf_op | source)
XLA Modules:
  0.0 59.0 jit_solution(18389818578500949141)
XLA Ops:
  0.6 57.0 %primal_dual.1 = (f32[4,256,128]{2,1,0:T(8,128)S(1)}, f32[4,256,128]{2,1,0:T(8,128)S(1)}, f32[4,256,128]{2,1,0:T(8,128)S(1)}, f32[4,256,128]{2,1,0:T(8,128)S(1)}, f32[256,128]{1,0:T(8,128)S(1)}) custom-call(f32[4,256,128]{2,1,0:T(8,128)} %bitcast.13, f32[4,256,128]{2,1,0:T(8,128)} %bitcast.14, f32[4,256,128]{2,1,0:T(8,128)} %bitcast.15, ...), custom_call_target="tpu_custom_call" | custom-call | flops 1258291200 | bytes 6291456 | tf_op jit(solution)/shard_map/primal_dual/pallas_call | solution.py:415
  57.7 1.4 %finish.1 = (f32[4,256,128]{2,1,0:T(8,128)}, f32[4,256,128]{2,1,0:T(8,128)}, f32[4,256,128]{2,1,0:T(8,128)}, f32[4,256,128]{2,1,0:T(8,128)}) custom-call(f32[4,256,128]{2,1,0:T(8,128)S(1)} %get-tuple-element.13.v2, f32[4,256,128]{2,1,0:T(8,128)S(1)} %get-tuple-element.14.s2, f32[4,256,128]{2,1,0:T(8,128)S(1)} %get-tuple-element.15.y2, ...), custom_call_target="tpu_custom_call" | custom-call | tf_op jit(solution)/shard_map/finish/pallas_call | solution.py:435

commit v8 on v7

--- a/solution.py
+++ b/solution.py
@@ -9,7 +9,7 @@
 
 PANEL = 128
 ROWS = 4
-SHARES = (8, 8, 7, 6, 3)
+SHARES = (10, 8, 7, 5, 2)
 CHUNKS = len(SHARES)
 EARLY = 1
 LATE = 1

time: 59.4 us -> 61.4 us (1.034)
  Pallas kernels: 58.4 us -> 60.1 us
    pallas_call x1, Pallas kernels: 57 us -> 58.7 us  [shards(): pl.pallas_call(functools.partial(kernel, weeks, regions, panels), out_sha...]
where the time goes in v8:
time: 61.4 us; the launch traced here: 60.7 us
  Pallas kernels  60.1 us (98%)
  between operations  0.64 us (1%)
    pallas_call x1, Pallas kernels, shards(): pl.pallas_call(functools.partial(kernel, weeks, regions, panels), out_sha...  58.7 us
    pallas_call x1, Pallas kernels, shards(): pl.pallas_call(finish, out_shape=[jax.ShapeDtypeStruct(slab, F32)] * 4, i...  1.37 us

profile of v8, /device:TPU:2, one launch (start us, length us, event | category | flops | bytes accessed | tf_op | source)
XLA Modules:
  0.0 60.7 jit_solution(14012274555865997122)
XLA Ops:
  0.6 58.7 %primal_dual.1 = (f32[4,256,128]{2,1,0:T(8,128)S(1)}, f32[4,256,128]{2,1,0:T(8,128)S(1)}, f32[4,256,128]{2,1,0:T(8,128)S(1)}, f32[4,256,128]{2,1,0:T(8,128)S(1)}, f32[256,128]{1,0:T(8,128)S(1)}) custom-call(f32[4,256,128]{2,1,0:T(8,128)} %bitcast.13, f32[4,256,128]{2,1,0:T(8,128)} %bitcast.14, f32[4,256,128]{2,1,0:T(8,128)} %bitcast.15, ...), custom_call_target="tpu_custom_call" | custom-call | flops 1258291200 | bytes 6291456 | tf_op jit(solution)/shard_map/primal_dual/pallas_call | solution.py:415
  59.3 1.4 %finish.1 = (f32[4,256,128]{2,1,0:T(8,128)}, f32[4,256,128]{2,1,0:T(8,128)}, f32[4,256,128]{2,1,0:T(8,128)}, f32[4,256,128]{2,1,0:T(8,128)}) custom-call(f32[4,256,128]{2,1,0:T(8,128)S(1)} %get-tuple-element.13.v2, f32[4,256,128]{2,1,0:T(8,128)S(1)} %get-tuple-element.14.s2, f32[4,256,128]{2,1,0:T(8,128)S(1)} %get-tuple-element.15.y2, ...), custom_call_target="tpu_custom_call" | custom-call | tf_op jit(solution)/shard_map/finish/pallas_call | solution.py:435
